TPU v7x, 32 devices: a whole 2x2x4 slice. The times are simulated.
32 devices in a mesh: seq: 8 (over z, x), tp: 4 (over y, core).
Axes of the slice: x: 2, y: 2, z: 4, core: 2. Of those that a mesh axis runs over, the one named last changes fastest.
Arguments:
- tokens: bfloat16 [16384, 1024], P('seq'), may hold values from -6 to 6
- cotangent: bfloat16 [16384, 1024], P('seq'), may hold values from -6 to 6
- start_flags: int32 [8], P('seq'), may hold values from 0 to 1, as said below
- gain_mixer: float32 [1024], replicated, may hold values from 0.5 to 1.5
- w_bgate: bfloat16 [1024, 1024], P(None, 'tp'), may hold values from -0.1875 to 0.1875
- w_cgate: bfloat16 [1024, 1024], P(None, 'tp'), may hold values from -0.1875 to 0.1875
- w_input: bfloat16 [1024, 1024], P(None, 'tp'), may hold values from -0.1875 to 0.1875
- conv_kernel: bfloat16 [3, 1024], P(None, 'tp'), may hold values from -3.5 to 3.5
- w_output: bfloat16 [1024, 1024], P('tp'), may hold values from -0.1875 to 0.1875
- gain_ffn: float32 [1024], replicated, may hold values from 0.5 to 1.5
- w_gate: bfloat16 [1024, 4608], P(None, 'tp'), may hold values from -0.1875 to 0.1875
- w_up: bfloat16 [1024, 4608], P(None, 'tp'), may hold values from -0.1875 to 0.1875
- w_down: bfloat16 [4608, 1024], P('tp'), may hold values from -0.09375 to 0.09375
- mean_gain_mixer: float32 [1024], replicated, may hold values from -16 to 16
- square_gain_mixer: float32 [1024], replicated, may hold values from 1 to 100
- mean_w_bgate: float32 [1024, 1024], P('seq', 'tp'), may hold values from -16 to 16
- square_w_bgate: float32 [1024, 1024], P('seq', 'tp'), may hold values from 1 to 100
- mean_w_cgate: float32 [1024, 1024], P('seq', 'tp'), may hold values from -16 to 16
- square_w_cgate: float32 [1024, 1024], P('seq', 'tp'), may hold values from 1 to 100
- mean_w_input: float32 [1024, 1024], P('seq', 'tp'), may hold values from -16 to 16
- square_w_input: float32 [1024, 1024], P('seq', 'tp'), may hold values from 1 to 100
- mean_conv_kernel: float32 [3, 1024], P(None, 'tp'), may hold values from -16 to 16
- square_conv_kernel: float32 [3, 1024], P(None, 'tp'), may hold values from 1 to 100
- mean_w_output: float32 [1024, 1024], P('tp', 'seq'), may hold values from -16 to 16
- square_w_output: float32 [1024, 1024], P('tp', 'seq'), may hold values from 1 to 100
- mean_gain_ffn: float32 [1024], replicated, may hold values from -16 to 16
- square_gain_ffn: float32 [1024], replicated, may hold values from 1 to 100
- mean_w_gate: float32 [1024, 4608], P('seq', 'tp'), may hold values from -16 to 16
- square_w_gate: float32 [1024, 4608], P('seq', 'tp'), may hold values from 1 to 100
- mean_w_up: float32 [1024, 4608], P('seq', 'tp'), may hold values from -16 to 16
- square_w_up: float32 [1024, 4608], P('seq', 'tp'), may hold values from 1 to 100
- mean_w_down: float32 [4608, 1024], P('tp', 'seq'), may hold values from -16 to 16
- square_w_down: float32 [4608, 1024], P('tp', 'seq'), may hold values from 1 to 100
Outputs:
- block_out: bfloat16 [16384, 1024], P('seq')
- grad_tokens: float32 [16384, 1024], P('seq')
- grad_gain_mixer: float32 [1024], replicated
- next_gain_mixer: float32 [1024], replicated
- mean_next_gain_mixer: float32 [1024], replicated
- square_next_gain_mixer: float32 [1024], replicated
- grad_w_bgate: float32 [1024, 1024], P('seq', 'tp')
- next_w_bgate: float32 [1024, 1024], P('seq', 'tp')
- mean_next_w_bgate: float32 [1024, 1024], P('seq', 'tp')
- square_next_w_bgate: float32 [1024, 1024], P('seq', 'tp')
- grad_w_cgate: float32 [1024, 1024], P('seq', 'tp')
- next_w_cgate: float32 [1024, 1024], P('seq', 'tp')
- mean_next_w_cgate: float32 [1024, 1024], P('seq', 'tp')
- square_next_w_cgate: float32 [1024, 1024], P('seq', 'tp')
- grad_w_input: float32 [1024, 1024], P('seq', 'tp')
- next_w_input: float32 [1024, 1024], P('seq', 'tp')
- mean_next_w_input: float32 [1024, 1024], P('seq', 'tp')
- square_next_w_input: float32 [1024, 1024], P('seq', 'tp')
- grad_conv_kernel: float32 [3, 1024], P(None, 'tp')
- next_conv_kernel: float32 [3, 1024], P(None, 'tp')
- mean_next_conv_kernel: float32 [3, 1024], P(None, 'tp')
- square_next_conv_kernel: float32 [3, 1024], P(None, 'tp')
- grad_w_output: float32 [1024, 1024], P('tp', 'seq')
- next_w_output: float32 [1024, 1024], P('tp', 'seq')
- mean_next_w_output: float32 [1024, 1024], P('tp', 'seq')
- square_next_w_output: float32 [1024, 1024], P('tp', 'seq')
- grad_gain_ffn: float32 [1024], replicated
- next_gain_ffn: float32 [1024], replicated
- mean_next_gain_ffn: float32 [1024], replicated
- square_next_gain_ffn: float32 [1024], replicated
- grad_w_gate: float32 [1024, 4608], P('seq', 'tp')
- next_w_gate: float32 [1024, 4608], P('seq', 'tp')
- mean_next_w_gate: float32 [1024, 4608], P('seq', 'tp')
- square_next_w_gate: float32 [1024, 4608], P('seq', 'tp')
- grad_w_up: float32 [1024, 4608], P('seq', 'tp')
- next_w_up: float32 [1024, 4608], P('seq', 'tp')
- mean_next_w_up: float32 [1024, 4608], P('seq', 'tp')
- square_next_w_up: float32 [1024, 4608], P('seq', 'tp')
- grad_w_down: float32 [4608, 1024], P('tp', 'seq')
- next_w_down: float32 [4608, 1024], P('tp', 'seq')
- mean_next_w_down: float32 [4608, 1024], P('tp', 'seq')
- square_next_w_down: float32 [4608, 1024], P('tp', 'seq')
Inputs may be any that keep to these rules, and one draw needn't show every extreme that they name: `start_flags`: the first shard's flag is 1; shards 1 and 5 have flag 0, so they continue the sequence of the shard before them.
All inputs are finite; a program needn't handle non-finite values.
Results may differ from a plain program's by a relative error of at most 0.0075.
The roundings to bfloat16 on the way count: a program that leaves them out, or rounds other values in their place, can miss the bound.
Values sent between devices are 32-bit elements; how exact they have to be, the bound alone decides.
No kernel may reach another device: no remote copies, remote signals or barrier semaphores. Data moves between devices by JAX's collectives and lax.ppermute only.
A program may use at most 192 MiB of HBM per device.

v0:
```python
import jax
import jax.numpy as jnp
from jax import lax
from jax.sharding import PartitionSpec as P

EPS = 1e-05


def shifted(block, axis, distance):
    devices = range(lax.axis_size(axis))
    route = [(i - distance, i) for i in devices if i - distance in devices]
    return lax.ppermute(block, axis, route)


def inner_rows(left, right):
    return lax.dot_general(
        left, right, (((0,), (0,)), ((), ())), preferred_element_type=jnp.float32
    )


def times_back(left, right):
    return lax.dot_general(
        left, right, (((1,), (1,)), ((), ())), preferred_element_type=jnp.float32
    )


def adamw(weight, grad, mean, square, decay, rate):
    mean_new = 0.9 * mean + 0.1 * grad
    square_new = 0.95 * square + 0.05 * grad * grad
    mean_hat = mean_new / (1.0 - 0.9**3)
    square_hat = square_new / (1.0 - 0.95**3)
    weight_new = weight - rate * (mean_hat / (jnp.sqrt(square_hat) + 1e-08) + decay * weight)
    return (weight_new, mean_new, square_new)


def norm_back(dnormed, normed, inverse):
    return inverse * (dnormed - normed * jnp.mean(dnormed * normed, axis=-1, keepdims=True))


def body(
    tokens,
    cotangent,
    start_flags,
    gain_mixer,
    w_bgate,
    w_cgate,
    w_input,
    conv_kernel,
    w_output,
    gain_ffn,
    w_gate,
    w_up,
    w_down,
    mean_gain_mixer,
    square_gain_mixer,
    mean_w_bgate,
    square_w_bgate,
    mean_w_cgate,
    square_w_cgate,
    mean_w_input,
    square_w_input,
    mean_conv_kernel,
    square_conv_kernel,
    mean_w_output,
    square_w_output,
    mean_gain_ffn,
    square_gain_ffn,
    mean_w_gate,
    square_w_gate,
    mean_w_up,
    square_w_up,
    mean_w_down,
    square_w_down,
):
    count = tokens.shape[0]
    xin = tokens.astype(jnp.float32)
    inverse_one = lax.rsqrt(jnp.mean(xin * xin, axis=-1, keepdims=True) + EPS)
    norm_one = xin * inverse_one
    hone = (norm_one * gain_mixer).astype(jnp.bfloat16)
    bgate = jnp.dot(hone, w_bgate, preferred_element_type=jnp.float32)
    cgate = jnp.dot(hone, w_cgate, preferred_element_type=jnp.float32)
    xval = jnp.dot(hone, w_input, preferred_element_type=jnp.float32)
    mixed_in = bgate * xval
    keeper = (1 - start_flags[0]).astype(jnp.float32)
    kernel = conv_kernel.astype(jnp.float32)
    previous = shifted(mixed_in[-2:], "seq", 1) * keeper
    extended = jnp.concatenate([previous, mixed_in], axis=0)
    conv = kernel[2] * mixed_in + kernel[1] * extended[1:-1] + kernel[0] * extended[:-2]
    gated = (cgate * conv).astype(jnp.bfloat16)
    mix = lax.psum(jnp.dot(gated, w_output, preferred_element_type=jnp.float32), "tp")
    resid = xin + mix
    inverse_two = lax.rsqrt(jnp.mean(resid * resid, axis=-1, keepdims=True) + EPS)
    norm_two = resid * inverse_two
    htwo = (norm_two * gain_ffn).astype(jnp.bfloat16)
    gate = jnp.dot(htwo, w_gate, preferred_element_type=jnp.float32)
    upval = jnp.dot(htwo, w_up, preferred_element_type=jnp.float32)
    sigma = jax.nn.sigmoid(gate)
    silu_gate = gate * sigma
    act = (silu_gate * upval).astype(jnp.bfloat16)
    ffn = lax.psum(jnp.dot(act, w_down, preferred_element_type=jnp.float32), "tp")
    block_out = (resid + ffn).astype(jnp.bfloat16)
    gout = cotangent.astype(jnp.float32)
    grad_down = inner_rows(act, cotangent)
    dact = times_back(cotangent, w_down)
    dgate = (dact * upval * (sigma * (1.0 + gate * (1.0 - sigma)))).astype(jnp.bfloat16)
    dupval = (dact * silu_gate).astype(jnp.bfloat16)
    grad_gate = inner_rows(htwo, dgate)
    grad_upw = inner_rows(htwo, dupval)
    dhtwo_part = times_back(dgate, w_gate) + times_back(dupval, w_up)
    dhtwo = lax.psum(dhtwo_part, "tp")
    dgain_ffn = jnp.sum(dhtwo * norm_two, axis=0)
    dresid = gout + norm_back(dhtwo * gain_ffn, norm_two, inverse_two)
    dmix = dresid.astype(jnp.bfloat16)
    grad_outw = inner_rows(gated, dmix)
    dgated = times_back(dmix, w_output)
    dcgate = (dgated * conv).astype(jnp.bfloat16)
    dconv = dgated * cgate
    dkernel = jnp.stack(
        [
            jnp.sum(dconv * extended[:-2], axis=0),
            jnp.sum(dconv * extended[1:-1], axis=0),
            jnp.sum(dconv * mixed_in, axis=0),
        ],
        axis=0,
    )
    dextended = (
        jnp.pad(kernel[2] * dconv, ((2, 0), (0, 0)))
        + jnp.pad(kernel[1] * dconv, ((1, 1), (0, 0)))
        + jnp.pad(kernel[0] * dconv, ((0, 2), (0, 0)))
    )
    returned = shifted(dextended[:2] * keeper, "seq", -1)
    dmixed = dextended[2:] + jnp.pad(returned, ((count - 2, 0), (0, 0)))
    dbgate = (dmixed * xval).astype(jnp.bfloat16)
    dxval = (dmixed * bgate).astype(jnp.bfloat16)
    grad_bw = inner_rows(hone, dbgate)
    grad_cw = inner_rows(hone, dcgate)
    grad_xw = inner_rows(hone, dxval)
    shared = (
        lax.psum_scatter(grad_bw, "seq", scatter_dimension=0, tiled=True),
        lax.psum_scatter(grad_cw, "seq", scatter_dimension=0, tiled=True),
        lax.psum_scatter(grad_xw, "seq", scatter_dimension=0, tiled=True),
        lax.psum_scatter(grad_outw, "seq", scatter_dimension=1, tiled=True),
        lax.psum_scatter(grad_gate, "seq", scatter_dimension=0, tiled=True),
        lax.psum_scatter(grad_upw, "seq", scatter_dimension=0, tiled=True),
        lax.psum_scatter(grad_down, "seq", scatter_dimension=1, tiled=True),
    )
    dhone_part = (
        times_back(dbgate, w_bgate) + times_back(dcgate, w_cgate) + times_back(dxval, w_input)
    )
    dhone = lax.psum(dhone_part, "tp")
    dgain_mixer = jnp.sum(dhone * norm_one, axis=0)
    grad_tokens = dresid + norm_back(dhone * gain_mixer, norm_one, inverse_one)
    small = lax.psum((dgain_mixer, dgain_ffn, dkernel), "seq")
    width = w_bgate.shape[0] // lax.axis_size("seq")
    offset = lax.axis_index("seq") * width

    def rows_of(weight):
        return lax.dynamic_slice_in_dim(weight, offset, width, 0).astype(jnp.float32)

    def columns_of(weight):
        return lax.dynamic_slice_in_dim(weight, offset, width, 1).astype(jnp.float32)

    params = [
        gain_mixer,
        rows_of(w_bgate),
        rows_of(w_cgate),
        rows_of(w_input),
        kernel,
        columns_of(w_output),
        gain_ffn,
        rows_of(w_gate),
        rows_of(w_up),
        columns_of(w_down),
    ]
    grads = [
        small[0],
        shared[0],
        shared[1],
        shared[2],
        small[2],
        shared[3],
        small[1],
        shared[4],
        shared[5],
        shared[6],
    ]
    moments = [
        (mean_gain_mixer, square_gain_mixer),
        (mean_w_bgate, square_w_bgate),
        (mean_w_cgate, square_w_cgate),
        (mean_w_input, square_w_input),
        (mean_conv_kernel, square_conv_kernel),
        (mean_w_output, square_w_output),
        (mean_gain_ffn, square_gain_ffn),
        (mean_w_gate, square_w_gate),
        (mean_w_up, square_w_up),
        (mean_w_down, square_w_down),
    ]
    decays = [0.0, 0.1, 0.1, 0.1, 0.1, 0.1, 0.0, 0.1, 0.1, 0.1]
    rates = [0.2, 0.01, 0.01, 0.01, 0.2, 0.01, 0.2, 0.01, 0.01, 0.01]
    outs = [block_out, grad_tokens]
    for index in range(10):
        weight_new, mean_new, square_new = adamw(
            params[index],
            grads[index],
            moments[index][0],
            moments[index][1],
            decays[index],
            rates[index],
        )
        outs = outs + [grads[index], weight_new, mean_new, square_new]
    return tuple(outs)


def solution(mesh):
    in_specs = (
        P("seq", None),
        P("seq", None),
        P("seq"),
        P(),
        P(None, "tp"),
        P(None, "tp"),
        P(None, "tp"),
        P(None, "tp"),
        P("tp", None),
        P(),
        P(None, "tp"),
        P(None, "tp"),
        P("tp", None),
        P(),
        P(),
        P("seq", "tp"),
        P("seq", "tp"),
        P("seq", "tp"),
        P("seq", "tp"),
        P("seq", "tp"),
        P("seq", "tp"),
        P(None, "tp"),
        P(None, "tp"),
        P("tp", "seq"),
        P("tp", "seq"),
        P(),
        P(),
        P("seq", "tp"),
        P("seq", "tp"),
        P("seq", "tp"),
        P("seq", "tp"),
        P("tp", "seq"),
        P("tp", "seq"),
    )
    out_specs = (
        P("seq", None),
        P("seq", None),
        P(),
        P(),
        P(),
        P(),
        P("seq", "tp"),
        P("seq", "tp"),
        P("seq", "tp"),
        P("seq", "tp"),
        P("seq", "tp"),
        P("seq", "tp"),
        P("seq", "tp"),
        P("seq", "tp"),
        P("seq", "tp"),
        P("seq", "tp"),
        P("seq", "tp"),
        P("seq", "tp"),
        P(None, "tp"),
        P(None, "tp"),
        P(None, "tp"),
        P(None, "tp"),
        P("tp", "seq"),
        P("tp", "seq"),
        P("tp", "seq"),
        P("tp", "seq"),
        P(),
        P(),
        P(),
        P(),
        P("seq", "tp"),
        P("seq", "tp"),
        P("seq", "tp"),
        P("seq", "tp"),
        P("seq", "tp"),
        P("seq", "tp"),
        P("seq", "tp"),
        P("seq", "tp"),
        P("tp", "seq"),
        P("tp", "seq"),
        P("tp", "seq"),
        P("tp", "seq"),
    )
    return jax.shard_map(body, mesh=mesh, in_specs=in_specs, out_specs=out_specs, check_vma=False)
```

profile of v0, /device:TPU:0, one launch (start us, length us, event | category | flops | bytes accessed | tf_op | source)
XLA Modules:
  0.0 1340.3 jit_solution(14432429471371438521)
XLA Ops:
  16.3 4.8 collective-permute-start
  22.5 3.6 multiply_convert_fusion.7
  26.1 4.7 fusion.54
  31.3 154.5 %all-reduce.10.cloned.1.call-done = f32[2048,1024]{1,0:T(8,128)} async-done(((f32[2048,1024]{1,0:T(8,128)}), f32[2048,1024]{1,0:T(8,128)}) %all-reduce.10.cloned.1.call-update) | async-done | bytes 8388624 | tf_op jit(solution)/shard_map/psum | solution.py:90
  185.8 5.7 multiply_reduce_fusion.2
  195.2 7.9 fusion.56
  203.1 7.9 fusion.55
  211.0 17.9 %multiply_convert_fusion = (bf16[2048,1152]{1,0:T(8,128)(2,1)}, bf16[2048,1152]{1,0:T(8,128)(2,1)}, bf16[2048,1152]{1,0:T(8,128)(2,1)}) fusion(f32[2048,1152]{1,0:T(8,128)} %fusion.55, f32[2048,1152]{1,0:T(8,128)} %fusion.56, bf16[2048,1024]{1,0:T(8,128)(2,1)} %param.34, bf16[1152,1024]{1,0:T(8,128)(2,1)} %param.45), kind=kOutput, calls=%fused_computation.7 | convolution fusion | flops 4867227648 | bytes 39583744 | tf_op jit(solution)/shard_map/dot_general | solution.py:22
  228.9 7.7 fusion.58
  236.6 8.4 convolution_add_fusion
  245.1 153.1 %all-reduce.12.cloned.1.call-done = f32[2048,1024]{1,0:T(8,128)} async-done(((f32[2048,1024]{1,0:T(8,128)}), f32[2048,1024]{1,0:T(8,128)}) %all-reduce.12.cloned.1.call-update) | async-done | bytes 8388624 | tf_op jit(solution)/shard_map/psum | solution.py:110
  398.2 7.1 multiply_reduce_fusion
  407.6 4.5 multiply_add_fusion
  412.2 3.4 copy-done.1
  417.9 4.9 fusion.15
  430.9 3.5 collective-permute-done.1
  439.0 4.5 fusion.61
  443.6 10.3 fusion.64
  453.9 10.3 fusion.65
  464.4 9.7 fusion.66
  474.4 10.2 fusion.57
  487.3 4.7 add_add_fusion
  494.7 54.1 %reduce-scatter.10.cloned.1.call-done = f32[128,256]{1,0:T(8,128)} async-done(((f32[1024,256]{1,0:T(8,128)}), f32[128,256]{1,0:T(8,128)}) %reduce-scatter.10.cloned.1.call-update) | async-done | bytes 131088 | tf_op jit(solution)/shard_map/reduce_scatter | solution.py:140
  550.5 64.5 %reduce-scatter.12.cloned.1.call-done = f32[128,256]{1,0:T(8,128)} async-done(((f32[1024,256]{1,0:T(8,128)}), f32[128,256]{1,0:T(8,128)}) %reduce-scatter.12.cloned.1.call-update) | async-done | bytes 131088 | tf_op jit(solution)/shard_map/reduce_scatter | solution.py:141
  616.8 64.9 %reduce-scatter.8.cloned.1.call-done = f32[128,256]{1,0:T(8,128)} async-done(((f32[1024,256]{1,0:T(8,128)}), f32[128,256]{1,0:T(8,128)}) %reduce-scatter.8.cloned.1.call-update) | async-done | bytes 131088 | tf_op jit(solution)/shard_map/reduce_scatter | solution.py:139
  683.6 96.8 %reduce-scatter.16.cloned.1.call-done = f32[128,1152]{1,0:T(8,128)} async-done(((f32[1024,1152]{1,0:T(8,128)}), f32[128,1152]{1,0:T(8,128)}) %reduce-scatter.16.cloned.1.call-update) | async-done | bytes 589840 | tf_op jit(solution)/shard_map/reduce_scatter | solution.py:143
  783.1 96.8 %reduce-scatter.18.cloned.1.call-done = f32[128,1152]{1,0:T(8,128)} async-done(((f32[1024,1152]{1,0:T(8,128)}), f32[128,1152]{1,0:T(8,128)}) %reduce-scatter.18.cloned.1.call-update) | async-done | bytes 589840 | tf_op jit(solution)/shard_map/reduce_scatter | solution.py:144
  882.5 97.0 %reduce-scatter.20.cloned.1.call-done = f32[1152,128]{1,0:T(8,128)} async-done(((f32[1152,1024]{1,0:T(8,128)}), f32[1152,128]{1,0:T(8,128)}) %reduce-scatter.20.cloned.1.call-update) | async-done | bytes 589840 | tf_op jit(solution)/shard_map/reduce_scatter | solution.py:145
  982.3 288.3 %all-reduce.14.cloned.1.call-done = (f32[2048,1024]{1,0:T(8,128)}, f32[2048,1024]{1,0:T(8,128)}) async-done(((f32[2048,1024]{1,0:T(8,128)}, f32[2048,1024]{1,0:T(8,128)}), (f32[2048,1024]{1,0:T(8,128)}, f32[2048,1024]{1,0:T(8,128)})) %all-reduce.14.cloned.1.call-update) | async-done | bytes 16777232 | tf_op jit(solution)/shard_map/psum | solution.py:100
  1270.6 6.5 fusion.10
  1277.2 17.5 %fusion.9 = (f32[2048,1024]{1,0:T(8,128)}, bf16[2048,1024]{1,0:T(8,128)(2,1)}) fusion(f32[2048,1024]{1,0:T(8,128)} %copy-done.1, bf16[2048,1024]{1,0:T(8,128)(2,1)S(1)} %copy-done.3, f32[2048,1024]{1,0:T(8,128)} %get-tuple-element.53, f32[2048]{0:T(1024)S(1)} %broadcast_multiply_fusion.3, f32[1024]{0:T(1024)S(1)} %copy-done.36, f32[2048]{0:T(1024)S(1)} %copy-done.33, ...), kind=kLoop, calls=%fused_computation.16 | loop fusion | flops 18874368 | bytes 50352128 | tf_op jit(solution)/shard_map/add | solution.py:152
  1294.7 37.1 %all-reduce.4 = (f32[1024]{0:T(1024)S(1)}, f32[3,256]{1,0:T(4,128)S(1)}, f32[1024]{0:T(1024)S(1)}) all-reduce(f32[1024]{0:T(1024)S(1)} %get-tuple-element.44, f32[3,256]{1,0:T(4,128)S(1)} %pad_maximum_fusion.1, f32[1024]{0:T(1024)S(1)} %get-tuple-element.42), channel_id=1, replica_groups=mesh['seq'=8,'tp'=4] {'seq'}, use_global_device_ids=true, to_apply=%region_9.0 | all-reduce | flops 2816 | bytes 22528 | tf_op jit(solution)/shard_map/psum | solution.py:153
  (160 shorter events, 51.7 us)
Async XLA Ops:
  7.2 178.6 %all-reduce.10.cloned.1.call-start = ((), (), s32[]{:S(2)}) async-start(), calls=%async_computation.7 | async-start | bytes 16777216 | tf_op jit(solution)/shard_map/psum | solution.py:90
  12.3 10.2 copy-start.5
  16.3 6.1 collective-permute-start
  30.7 160.8 %copy-start.34 = (f32[1024]{0:T(1024)S(1)}, f32[1024]{0:T(1024)}, u32[]{:S(2)}) copy-start(f32[1024]{0:T(1024)} %param.42) | copy-start | bytes 12292
  30.7 367.5 %all-reduce.12.cloned.1.call-start = ((), (), s32[]{:S(2)}) async-start(), calls=%async_computation.8 | async-start | bytes 16777216 | tf_op jit(solution)/shard_map/psum | solution.py:110
  211.0 17.9 %copy-start.38 = (bf16[1024,1152]{1,0:T(8,128)(2,1)S(1)}, bf16[1024,1152]{1,0:T(8,128)(2,1)}, u32[]{:S(2)}) copy-start(bf16[1024,1152]{1,0:T(8,128)(2,1)} %param.43) | copy-start | bytes 7077892
  245.1 247.0 %reduce-scatter.14.cloned.1.call-start = ((), (), s32[]{:S(2)}) async-start(), calls=%async_computation.12 | async-start | bytes 1179648 | tf_op jit(solution)/shard_map/reduce_scatter | solution.py:142
  417.8 130.9 %reduce-scatter.10.cloned.1.call-start = ((), (), s32[]{:S(2)}) async-start(), calls=%async_computation.10 | async-start | bytes 1179648 | tf_op jit(solution)/shard_map/reduce_scatter | solution.py:140
  428.1 186.9 %reduce-scatter.12.cloned.1.call-start = ((), (), s32[]{:S(2)}) async-start(), calls=%async_computation.11 | async-start | bytes 1179648 | tf_op jit(solution)/shard_map/reduce_scatter | solution.py:141
  428.7 5.7 collective-permute-start.1
  438.9 242.8 %reduce-scatter.8.cloned.1.call-start = ((), (), s32[]{:S(2)}) async-start(), calls=%async_computation.9 | async-start | bytes 1179648 | tf_op jit(solution)/shard_map/reduce_scatter | solution.py:139
  443.5 336.9 %reduce-scatter.16.cloned.1.call-start = ((), (), s32[]{:S(2)}) async-start(), calls=%async_computation.13 | async-start | bytes 5308416 | tf_op jit(solution)/shard_map/reduce_scatter | solution.py:143
  453.9 425.9 %reduce-scatter.18.cloned.1.call-start = ((), (), s32[]{:S(2)}) async-start(), calls=%async_computation.14 | async-start | bytes 5308416 | tf_op jit(solution)/shard_map/reduce_scatter | solution.py:144
  464.3 515.2 %reduce-scatter.20.cloned.1.call-start = ((), (), s32[]{:S(2)}) async-start(), calls=%async_computation.15 | async-start | bytes 5308416 | tf_op jit(solution)/shard_map/reduce_scatter | solution.py:145
  474.1 796.5 %all-reduce.14.cloned.1.call-start = ((), (), s32[]{:S(2)}) async-start(), calls=%async_computation.16 | async-start | bytes 33554432 | tf_op jit(solution)/shard_map/psum | solution.py:100
  474.4 10.2 copy-start.20
  492.0 56.8 %copy-start.30 = (f32[128,256]{1,0:T(8,128)S(1)}, f32[128,256]{1,0:T(8,128)}, u32[]{:S(2)}) copy-start(f32[128,256]{1,0:T(8,128)} %param.50) | copy-start | bytes 393220
  492.0 56.8 %copy-start.31 = (f32[128,256]{1,0:T(8,128)S(1)}, f32[128,256]{1,0:T(8,128)}, u32[]{:S(2)}) copy-start(f32[128,256]{1,0:T(8,128)} %param.51) | copy-start | bytes 393220
  492.0 288.4 %copy-start.23 = (f32[128,1152]{1,0:T(8,128)S(1)}, f32[128,1152]{1,0:T(8,128)}, u32[]{:S(2)}) copy-start(f32[128,1152]{1,0:T(8,128)} %param.60) | copy-start | bytes 1769476
  492.0 288.4 %copy-start.24 = (f32[128,1152]{1,0:T(8,128)S(1)}, f32[128,1152]{1,0:T(8,128)}, u32[]{:S(2)}) copy-start(f32[128,1152]{1,0:T(8,128)} %param.61) | copy-start | bytes 1769476
  492.0 387.8 %copy-start.25 = (f32[128,1152]{1,0:T(8,128)S(1)}, f32[128,1152]{1,0:T(8,128)}, u32[]{:S(2)}) copy-start(f32[128,1152]{1,0:T(8,128)} %param.62) | copy-start | bytes 1769476
  492.0 387.8 %copy-start.26 = (f32[128,1152]{1,0:T(8,128)S(1)}, f32[128,1152]{1,0:T(8,128)}, u32[]{:S(2)}) copy-start(f32[128,1152]{1,0:T(8,128)} %param.63) | copy-start | bytes 1769476
  616.8 362.7 %copy-start.27 = (f32[1152,128]{1,0:T(8,128)S(1)}, f32[1152,128]{1,0:T(8,128)}, u32[]{:S(2)}) copy-start(f32[1152,128]{1,0:T(8,128)} %param.64) | copy-start | bytes 1769476
  783.1 487.5 %copy-start.33 = (f32[2048]{0:T(1024)S(1)}, f32[2048]{0:T(1024)}, u32[]{:S(2)}) copy-start(f32[2048]{0:T(1024)} %copy-done.32) | copy-start | bytes 24580
  783.1 487.5 %copy-start.36 = (f32[1024]{0:T(1024)S(1)}, f32[1024]{0:T(1024)}, u32[]{:S(2)}) copy-start(f32[1024]{0:T(1024)} %param.36) | copy-start | bytes 12292
  1277.1 54.6 %copy-start.42 = (bf16[3,256]{1,0:T(4,128)(2,1)S(1)}, bf16[3,256]{1,0:T(4,128)(2,1)}, u32[]{:S(2)}) copy-start(bf16[3,256]{1,0:T(4,128)(2,1)} %param.40) | copy-start | bytes 4612
  1277.2 54.6 %copy-start.49 = (f32[3,256]{1,0:T(4,128)S(1)}, f32[3,256]{1,0:T(4,128)}, u32[]{:S(2)}) copy-start(f32[3,256]{1,0:T(4,128)} %param.54) | copy-start | bytes 9220
  1277.2 54.6 %copy-start.50 = (f32[3,256]{1,0:T(4,128)S(1)}, f32[3,256]{1,0:T(4,128)}, u32[]{:S(2)}) copy-start(f32[3,256]{1,0:T(4,128)} %param.55) | copy-start | bytes 9220
  1277.2 55.2 %copy-start.43 = (f32[1024]{0:T(1024)S(1)}, f32[1024]{0:T(1024)}, u32[]{:S(2)}) copy-start(f32[1024]{0:T(1024)} %param.58) | copy-start | bytes 12292
  1277.2 55.2 %copy-start.44 = (f32[1024]{0:T(1024)S(1)}, f32[1024]{0:T(1024)}, u32[]{:S(2)}) copy-start(f32[1024]{0:T(1024)} %param.59) | copy-start | bytes 12292
  1277.2 55.2 %copy-start.45 = (f32[1024]{0:T(1024)S(1)}, f32[1024]{0:T(1024)}, u32[]{:S(2)}) copy-start(f32[1024]{0:T(1024)} %param.47) | copy-start | bytes 12292
  1277.2 55.2 %copy-start.46 = (f32[1024]{0:T(1024)S(1)}, f32[1024]{0:T(1024)}, u32[]{:S(2)}) copy-start(f32[1024]{0:T(1024)} %param.46) | copy-start | bytes 12292
  (33 other events, 136.6 us)
Sparse Core Ops, SparseCore 0:
  30.8 154.8 all-reduce.9
  245.2 152.9 all-reduce.11
  418.0 64.1 reduce-scatter.13
  486.4 62.3 reduce-scatter.9
  552.6 62.3 reduce-scatter.11
  619.2 62.4 reduce-scatter.7
  685.9 94.4 reduce-scatter.15
  784.6 95.1 reduce-scatter.17
  884.1 95.3 reduce-scatter.19
  982.0 288.5 all-reduce.13
where the time goes:
time: 1350 us; the launch traced here: 1340 us
  waiting for transfers between devices  1070 us (79%)
  matrix products  126 us (9%)
  other arithmetic  66.7 us (5%)
  blocking collectives  37.1 us (3%)
  between operations  15.9 us (1%)
    psum x1, waiting for transfers between devices, body(): lax.psum(jnp.dot(act, w_down, preferred_element_type=jnp.float32), 'tp')  288 us
    psum x1, waiting for transfers between devices, body(): lax.psum(jnp.dot(gated, w_output, preferred_element_type=jnp.float32), 'tp')  155 us
    psum x1, waiting for transfers between devices, body(): dhtwo = lax.psum(dhtwo_part, 'tp')  153 us
    reduce_scatter x1, waiting for transfers between devices, body(): lax.psum_scatter(grad_down, 'seq', scatter_dimension=1, tiled=True)  97 us
    reduce_scatter x1, waiting for transfers between devices, body(): lax.psum_scatter(grad_gate, 'seq', scatter_dimension=0, tiled=True)  96.8 us
    reduce_scatter x1, waiting for transfers between devices, body(): lax.psum_scatter(grad_upw, 'seq', scatter_dimension=0, tiled=True)  96.8 us
    reduce_scatter x1, waiting for transfers between devices, body(): lax.psum_scatter(grad_bw, 'seq', scatter_dimension=0, tiled=True)  64.9 us
    reduce_scatter x1, waiting for transfers between devices, body(): lax.psum_scatter(grad_xw, 'seq', scatter_dimension=0, tiled=True)  64.5 us
  transfers between devices with their start and end apart: 12, of which 11 were waited for; matrix products, arithmetic and copies ran while one was open for 6% of the time, Pallas kernels for 0%

commit v1 on v0

--- a/solution.py
+++ b/solution.py
@@ -10,6 +10,31 @@
     devices = range(lax.axis_size(axis))
     route = [(i - distance, i) for i in devices if i - distance in devices]
     return lax.ppermute(block, axis, route)
+
+
+def swap(block, axis, bit):
+    return lax.ppermute(block, axis, [(i, i ^ bit) for i in range(lax.axis_size(axis))])
+
+
+def swap_core(block):
+    return swap(block, "tp", 1)
+
+
+def swap_y(block):
+    return swap(block, "tp", 2)
+
+
+def narrow(block):
+    one = 1.0 + (lax.axis_index("tp") // lax.axis_size("tp")).astype(jnp.float32)
+    return (block * one).astype(jnp.bfloat16)
+
+
+def wide(block):
+    return block.astype(jnp.float32)
+
+
+def dot(left, right):
+    return jnp.dot(left, right, preferred_element_type=jnp.float32)
 
 
 def inner_rows(left, right):
@@ -35,6 +60,34 @@
 
 def norm_back(dnormed, normed, inverse):
     return inverse * (dnormed - normed * jnp.mean(dnormed * normed, axis=-1, keepdims=True))
+
+
+def log_two(number):
+    bits = number.bit_length() - 1
+    assert number == 1 << bits
+    return bits
+
+
+def scatter_rows(grad, place, order):
+    shards = lax.axis_size("seq")
+    width = grad.shape[0] // shards
+    total = grad.reshape((shards, width) + grad.shape[1:])
+    left = list(range(log_two(shards)))
+    for bit in order:
+        low = 1 << left.index(bit)
+        pairs = total.reshape((-1, 2, low) + total.shape[1:])
+        mine = (place >> bit) & 1
+        send = lax.dynamic_index_in_dim(pairs, 1 - mine, 1, keepdims=False)
+        keep = lax.dynamic_index_in_dim(pairs, mine, 1, keepdims=False)
+        total = (keep + swap(send, "seq", 1 << bit)).reshape((-1,) + total.shape[1:])
+        left.remove(bit)
+    return total[0]
+
+
+def sum_all(block, axis):
+    for bit in range(log_two(lax.axis_size(axis))):
+        block = block + swap(block, axis, 1 << bit)
+    return block
 
 
 def body(
@@ -72,47 +125,133 @@
     mean_w_down,
     square_w_down,
 ):
-    count = tokens.shape[0]
+    count, features = tokens.shape
+    part = count // 4
+    half = count // 2
+    place = lax.axis_index("seq")
+    rank = lax.axis_index("tp")
+    upper = rank // 2
+    near_first = list(range(log_two(lax.axis_size("seq"))))
+    far_first = [near_first[1], near_first[0]] + near_first[2:]
+
+    def rows(block, index, size):
+        return lax.dynamic_slice_in_dim(block, index * size, size, 0)
+
+    w_output_far = narrow(swap_y(wide(w_output)))
+    w_output_both = jnp.concatenate([w_output, w_output_far], axis=0)
     xin = tokens.astype(jnp.float32)
     inverse_one = lax.rsqrt(jnp.mean(xin * xin, axis=-1, keepdims=True) + EPS)
     norm_one = xin * inverse_one
     hone = (norm_one * gain_mixer).astype(jnp.bfloat16)
-    bgate = jnp.dot(hone, w_bgate, preferred_element_type=jnp.float32)
-    cgate = jnp.dot(hone, w_cgate, preferred_element_type=jnp.float32)
-    xval = jnp.dot(hone, w_input, preferred_element_type=jnp.float32)
-    mixed_in = bgate * xval
+    last = hone[-8:]
+    mixed_last = dot(last, w_bgate) * dot(last, w_input)
     keeper = (1 - start_flags[0]).astype(jnp.float32)
     kernel = conv_kernel.astype(jnp.float32)
-    previous = shifted(mixed_in[-2:], "seq", 1) * keeper
+    previous = shifted(mixed_last[-2:], "seq", 1) * keeper
+    bgate = dot(hone, w_bgate)
+    cgate = dot(hone, w_cgate)
+    xval = dot(hone, w_input)
+    mixed_in = bgate * xval
     extended = jnp.concatenate([previous, mixed_in], axis=0)
     conv = kernel[2] * mixed_in + kernel[1] * extended[1:-1] + kernel[0] * extended[:-2]
     gated = (cgate * conv).astype(jnp.bfloat16)
-    mix = lax.psum(jnp.dot(gated, w_output, preferred_element_type=jnp.float32), "tp")
-    resid = xin + mix
+
+    gated_far = narrow(swap_y(wide(rows(gated, 1 - upper, half))))
+    gated_both = jnp.concatenate([rows(gated, upper, half), gated_far], axis=1)
+    core = rank % 2
+    mix_send = dot(rows(gated_both, 1 - core, part), w_output_both)
+    mix_keep = dot(rows(gated_both, core, part), w_output_both)
+    x_own = rows(tokens, rank, part).astype(jnp.float32)
+    resid = x_own + (mix_keep + swap_core(mix_send))
     inverse_two = lax.rsqrt(jnp.mean(resid * resid, axis=-1, keepdims=True) + EPS)
     norm_two = resid * inverse_two
-    htwo = (norm_two * gain_ffn).astype(jnp.bfloat16)
-    gate = jnp.dot(htwo, w_gate, preferred_element_type=jnp.float32)
-    upval = jnp.dot(htwo, w_up, preferred_element_type=jnp.float32)
-    sigma = jax.nn.sigmoid(gate)
-    silu_gate = gate * sigma
-    act = (silu_gate * upval).astype(jnp.bfloat16)
-    ffn = lax.psum(jnp.dot(act, w_down, preferred_element_type=jnp.float32), "tp")
-    block_out = (resid + ffn).astype(jnp.bfloat16)
-    gout = cotangent.astype(jnp.float32)
-    grad_down = inner_rows(act, cotangent)
-    dact = times_back(cotangent, w_down)
-    dgate = (dact * upval * (sigma * (1.0 + gate * (1.0 - sigma)))).astype(jnp.bfloat16)
-    dupval = (dact * silu_gate).astype(jnp.bfloat16)
-    grad_gate = inner_rows(htwo, dgate)
-    grad_upw = inner_rows(htwo, dupval)
-    dhtwo_part = times_back(dgate, w_gate) + times_back(dupval, w_up)
-    dhtwo = lax.psum(dhtwo_part, "tp")
+    htwo_own = (norm_two * gain_ffn).astype(jnp.bfloat16)
+
+    sub = part // 2
+    htwo_wide = wide(htwo_own)
+    htwo_core = swap_core(htwo_wide)
+    far = [swap_y(htwo_wide[:sub]), swap_y(htwo_wide[sub:])]
+    cot = [rows(cotangent, rank ^ k, part) for k in range(4)]
+    blocks = [
+        (
+            jnp.concatenate([htwo_own, narrow(htwo_core)], axis=0),
+            jnp.concatenate([cot[0], cot[1]], axis=0),
+        )
+    ]
+    for j in range(2):
+        blocks.append(
+            (
+                jnp.concatenate([narrow(far[j]), narrow(swap_core(far[j]))], axis=0),
+                jnp.concatenate(
+                    [cot[2][j * sub : (j + 1) * sub], cot[3][j * sub : (j + 1) * sub]], axis=0
+                ),
+            )
+        )
+    acts, dgates, dups, ffns, dhtwos = [], [], [], [], []
+    for htwo, cots in blocks:
+        gate = dot(htwo, w_gate)
+        upval = dot(htwo, w_up)
+        sigma = jax.nn.sigmoid(gate)
+        silu_gate = gate * sigma
+        act = (silu_gate * upval).astype(jnp.bfloat16)
+        dact = times_back(cots, w_down)
+        dgate = (dact * upval * (sigma * (1.0 + gate * (1.0 - sigma)))).astype(jnp.bfloat16)
+        dup = (dact * silu_gate).astype(jnp.bfloat16)
+        acts.append(act)
+        dgates.append(dgate)
+        dups.append(dup)
+        size = htwo.shape[0] // 2
+        dsend = times_back(dgate[size:], w_gate) + times_back(dup[size:], w_up)
+        dkeep = times_back(dgate[:size], w_gate) + times_back(dup[:size], w_up)
+        dhtwos.append(dkeep + swap_core(dsend))
+        fsend = dot(act[size:], w_down)
+        fkeep = dot(act[:size], w_down)
+        ffns.append(fkeep + swap_core(fsend))
+    dhtwo = dhtwos[0] + jnp.concatenate([swap_y(dhtwos[1]), swap_y(dhtwos[2])], axis=0)
+    ffn = ffns[0] + jnp.concatenate([swap_y(ffns[1]), swap_y(ffns[2])], axis=0)
+    block_own = wide((resid + ffn).astype(jnp.bfloat16))
+
+    def gather(own):
+        beside = swap_core(own)
+        across = swap_y(own)
+        corner = swap_core(across)
+        pieces = [own, beside, across, corner]
+        whole = jnp.zeros((count, own.shape[1]), own.dtype)
+        for k in range(4):
+            whole = lax.dynamic_update_slice_in_dim(whole, pieces[k], (rank ^ k) * part, 0)
+        return whole
+
+    block_out = narrow(gather(block_own))
+
+    htwo_all = jnp.concatenate([b[0] for b in blocks], axis=0)
+    cot_all = jnp.concatenate([b[1] for b in blocks], axis=0)
+    act_all = jnp.concatenate(acts, axis=0)
+    dgate_all = jnp.concatenate(dgates, axis=0)
+    dup_all = jnp.concatenate(dups, axis=0)
+    grad_down = scatter_rows(inner_rows(cot_all, act_all), place, far_first)
+    grad_gate = scatter_rows(inner_rows(htwo_all, dgate_all), place, near_first)
+    grad_upw = scatter_rows(inner_rows(htwo_all, dup_all), place, near_first)
+
+    gout = rows(cotangent, rank, part).astype(jnp.float32)
     dgain_ffn = jnp.sum(dhtwo * norm_two, axis=0)
     dresid = gout + norm_back(dhtwo * gain_ffn, norm_two, inverse_two)
-    dmix = dresid.astype(jnp.bfloat16)
-    grad_outw = inner_rows(gated, dmix)
-    dgated = times_back(dmix, w_output)
+    dmix_own = dresid.astype(jnp.bfloat16)
+    dmix_core = narrow(swap_core(wide(dmix_own)))
+    dmix = jnp.where(
+        core == 0,
+        jnp.concatenate([dmix_own, dmix_core], axis=0),
+        jnp.concatenate([dmix_core, dmix_own], axis=0),
+    )
+    dgated_near = times_back(dmix, w_output)
+    dgated_far = swap_y(times_back(dmix, w_output_far))
+    dgated = jnp.where(
+        upper == 0,
+        jnp.concatenate([dgated_near, dgated_far], axis=0),
+        jnp.concatenate([dgated_far, dgated_near], axis=0),
+    )
+    grad_outw_both = scatter_rows(inner_rows(dmix, gated_both), place, near_first)
+    quarter = w_output.shape[0]
+    grad_outw = (grad_outw_both[:, :quarter] + swap_y(grad_outw_both[:, quarter:])).T
     dcgate = (dgated * conv).astype(jnp.bfloat16)
     dconv = dgated * cgate
     dkernel = jnp.stack(
@@ -132,33 +271,30 @@
     dmixed = dextended[2:] + jnp.pad(returned, ((count - 2, 0), (0, 0)))
     dbgate = (dmixed * xval).astype(jnp.bfloat16)
     dxval = (dmixed * bgate).astype(jnp.bfloat16)
-    grad_bw = inner_rows(hone, dbgate)
-    grad_cw = inner_rows(hone, dcgate)
-    grad_xw = inner_rows(hone, dxval)
-    shared = (
-        lax.psum_scatter(grad_bw, "seq", scatter_dimension=0, tiled=True),
-        lax.psum_scatter(grad_cw, "seq", scatter_dimension=0, tiled=True),
-        lax.psum_scatter(grad_xw, "seq", scatter_dimension=0, tiled=True),
-        lax.psum_scatter(grad_outw, "seq", scatter_dimension=1, tiled=True),
-        lax.psum_scatter(grad_gate, "seq", scatter_dimension=0, tiled=True),
-        lax.psum_scatter(grad_upw, "seq", scatter_dimension=0, tiled=True),
-        lax.psum_scatter(grad_down, "seq", scatter_dimension=1, tiled=True),
-    )
-    dhone_part = (
-        times_back(dbgate, w_bgate) + times_back(dcgate, w_cgate) + times_back(dxval, w_input)
-    )
-    dhone = lax.psum(dhone_part, "tp")
-    dgain_mixer = jnp.sum(dhone * norm_one, axis=0)
-    grad_tokens = dresid + norm_back(dhone * gain_mixer, norm_one, inverse_one)
-    small = lax.psum((dgain_mixer, dgain_ffn, dkernel), "seq")
-    width = w_bgate.shape[0] // lax.axis_size("seq")
-    offset = lax.axis_index("seq") * width
+    dall = jnp.concatenate([dbgate, dcgate, dxval], axis=1)
+    w_all = jnp.concatenate([w_bgate, w_cgate, w_input], axis=1)
+    dparts = [times_back(rows(dall, rank ^ k, part), w_all) for k in (3, 2, 1, 0)]
+    across = swap_y(dparts[1] + swap_core(dparts[0]))
+    dhone = dparts[3] + swap_core(dparts[2]) + across
+    grad_in = scatter_rows(inner_rows(hone, dall), place, near_first)
+    inverse_own = lax.rsqrt(jnp.mean(x_own * x_own, axis=-1, keepdims=True) + EPS)
+    norm_own = x_own * inverse_own
+    dgain_mixer = jnp.sum(dhone * norm_own, axis=0)
+    grad_own = dresid + norm_back(dhone * gain_mixer, norm_own, inverse_own)
+    grad_tokens = gather(grad_own)
+
+    gains = jnp.concatenate([dgain_mixer, dgain_ffn]).reshape(-1, 128)
+    small = sum_all(jnp.concatenate([gains, dkernel.reshape(-1, 128)], axis=0), "seq")
+    gains = sum_all(small[: gains.shape[0]], "tp").reshape(2, features)
+    dkernel = small[gains.size // 128 :].reshape(dkernel.shape)
+
+    width = features // lax.axis_size("seq")
 
     def rows_of(weight):
-        return lax.dynamic_slice_in_dim(weight, offset, width, 0).astype(jnp.float32)
+        return lax.dynamic_slice_in_dim(weight, place * width, width, 0).astype(jnp.float32)
 
     def columns_of(weight):
-        return lax.dynamic_slice_in_dim(weight, offset, width, 1).astype(jnp.float32)
+        return lax.dynamic_slice_in_dim(weight, place * width, width, 1).astype(jnp.float32)
 
     params = [
         gain_mixer,
@@ -173,16 +309,16 @@
         columns_of(w_down),
     ]
     grads = [
-        small[0],
-        shared[0],
-        shared[1],
-        shared[2],
-        small[2],
-        shared[3],
-        small[1],
-        shared[4],
-        shared[5],
-        shared[6],
+        gains[0],
+        grad_in[:, :quarter],
+        grad_in[:, quarter : 2 * quarter],
+        grad_in[:, 2 * quarter :],
+        dkernel,
+        grad_outw,
+        gains[1],
+        grad_gate,
+        grad_upw,
+        grad_down.T,
     ]
     moments = [
         (mean_gain_mixer, square_gain_mixer),

time: 1350 us -> 662 us (0.49)
  waiting for transfers between devices: 1070 us -> 323 us
  starting transfers between devices: 7.73 us -> 84.1 us
  local copies, waits for them, and re-layouts: 12.6 us -> 59.2 us
  blocking collectives: 37.1 us -> 0 us
  other arithmetic: 66.7 us -> 49.6 us
    psum x3 -> x0, waiting for transfers between devices: 596 us -> none  [the longest x1 288 us: body(): lax.psum(jnp.dot(act, w_down, preferred_element_type=jnp.float32), 'tp')]
    reduce_scatter x7 -> x0, waiting for transfers between devices: 474 us -> none  [the longest x1 97 us: body(): lax.psum_scatter(grad_down, 'seq', scatter_dimension=1, tiled=True)]
    ppermute x0 -> x50, waiting for transfers between devices: none -> 320 us  [swap(): lax.ppermute(block, axis, [(i, i ^ bit) for i in range(lax.axis_size(axis...]
    ppermute x0 -> x50, starting transfers between devices: none -> 77.7 us  [swap(): lax.ppermute(block, axis, [(i, i ^ bit) for i in range(lax.axis_size(axis...]
    psum x1 -> x0, blocking collectives: 37.1 us -> none  [body(): small = lax.psum((dgain_mixer, dgain_ffn, dkernel), 'seq')]
    dot_general x7 -> x19, matrix products: 38.2 us -> 62.2 us  [dot(): return jnp.dot(left, right, preferred_element_type=jnp.float32)]
    add x2 -> x15, other arithmetic: 22 us -> 3.65 us  [the longest x10 3.62 us: scatter_rows(): keep + swap(send, 'seq', 1 << bit)]
    reduce_sum x3 -> x2, other arithmetic: 19.3 us -> 1.2 us  [the longest x1 0.92 us: body(): dgain_mixer = jnp.sum(dhone * norm_own, axis=0)]
  transfers between devices with their start and end apart: 12 -> 52, of which waited for: 11 -> 23; matrix products, arithmetic and copies ran while one was open for 6% -> 29% of each run, Pallas kernels for 0% -> 0%
where the time goes in v1:
time: 662 us; the launch traced here: 653 us
  waiting for transfers between devices  323 us (49%)
  matrix products  133 us (20%)
  starting transfers between devices  84.1 us (13%)
  local copies, waits for them, and re-layouts  59.2 us (9%)
  other arithmetic  49.6 us (7%)
    ppermute x50, waiting for transfers between devices, swap(): lax.ppermute(block, axis, [(i, i ^ bit) for i in range(lax.axis_size(axis...  320 us
    ppermute x50, starting transfers between devices, swap(): lax.ppermute(block, axis, [(i, i ^ bit) for i in range(lax.axis_size(axis...  77.7 us
    dot_general x19, matrix products, dot(): return jnp.dot(left, right, preferred_element_type=jnp.float32)  62.2 us
    dot_general x21, matrix products, times_back(): lax.dot_general(left, right, (((1,), (1,)), ((), ())), preferred_element_...  46 us
    dot_general x5, matrix products, inner_rows(): lax.dot_general(left, right, (((0,), (0,)), ((), ())), preferred_element_...  25 us
    unnamed x240, local copies, waits for them, and re-layouts  20.9 us
    dynamic_update_slice x6, local copies, waits for them, and re-layouts, gather(): lax.dynamic_update_slice_in_dim(whole, pieces[k], (rank ^ k) * part, 0)  15.9 us
  transfers between devices with their start and end apart: 52, of which 23 were waited for; matrix products, arithmetic and copies ran while one was open for 29% of the time, Pallas kernels for 0%

profile of v1, /device:TPU:0, one launch (start us, length us, event | category | flops | bytes accessed | tf_op | source)
XLA Modules:
  0.0 652.8 jit_solution(14964008327471776896)
XLA Ops:
  18.7 7.9 %multiply_convert_fusion.16 = (bf16[2048,256]{1,0:T(8,128)(2,1)S(1)}, f32[2048,256]{1,0:T(8,128)}, f32[2048,256]{1,0:T(8,128)}) fusion(f32[2048,256]{1,0:T(8,128)} %get-tuple-element.198, f32[2,256]{1,0:T(2,128)S(1)} %broadcast_multiply_fusion.5, f32[256]{0:T(256)S(1)} %bitcast.156, f32[256]{0:T(256)S(1)} %bitcast.154, f32[256]{0:T(256)S(1)} %bitcast.152, ...), kind=kOutput, calls=%fused_computation.88 | convolution fusion | flops 1078460416 | bytes 12063744 | tf_op jit(solution)/shard_map/dot_general | solution.py:37
  28.2 9.9 %collective-permute-done.2 = f32[256,1024]{1,0:T(8,128)} collective-permute-done((f32[256,1024]{1,0:T(8,128)}, f32[256,1024]{1,0:T(8,128)}, u32[]{:S(2)}, u32[]{:S(2)}) %collective-permute-start.2) | collective-permute-done | bytes 1048608 | tf_op jit(solution)/shard_map/ppermute | solution.py:16
  39.4 19.7 %collective-permute-done.1 = f32[1024,256]{1,0:T(8,128)} collective-permute-done((f32[1024,256]{1,0:T(8,128)}, f32[1024,256]{1,0:T(8,128)}, u32[]{:S(2)}, u32[]{:S(2)}) %collective-permute-start.1) | collective-permute-done | bytes 1048608 | tf_op jit(solution)/shard_map/ppermute | solution.py:16
  82.2 5.0 fusion.56
  93.4 5.6 fusion.36
  99.1 14.4 %collective-permute-done.6 = f32[256,1024]{1,0:T(8,128)S(1)} collective-permute-done((f32[256,1024]{1,0:T(8,128)S(1)}, f32[256,1024]{1,0:T(8,128)S(1)}, u32[]{:S(2)}, u32[]{:S(2)}) %collective-permute-start.6) | collective-permute-done | bytes 1048608 | tf_op jit(solution)/shard_map/ppermute | solution.py:16
  113.5 21.6 %collective-permute-done.10 = f32[256,1024]{1,0:T(8,128)S(1)} collective-permute-done((f32[256,1024]{1,0:T(8,128)S(1)}, f32[256,1024]{1,0:T(8,128)S(1)}, u32[]{:S(2)}, u32[]{:S(2)}) %collective-permute-start.10) | collective-permute-done | bytes 1048608 | tf_op jit(solution)/shard_map/ppermute | solution.py:16
  139.3 5.3 fusion.43
  147.2 8.9 %multiply_convert_fusion.1 = (bf16[1024,1152]{1,0:T(8,128)(2,1)S(1)}, bf16[1024,1152]{1,0:T(8,128)(2,1)}, bf16[1024,1152]{1,0:T(8,128)(2,1)S(1)}) fusion(f32[1024,1152]{1,0:T(8,128)} %fusion.36, f32[1024,1152]{1,0:T(8,128)} %fusion.43, bf16[1024,1152]{1,0:T(8,128)(2,1)S(1)} %copy-done.6, bf16[512,1024]{1,0:T(8,128)(2,1)S(1)} %get-tuple-element.124, ...), kind=kOutput, calls=%fused_computation.24 | convolution fusion | flops 2437808128 | bytes 20971520 | tf_op jit(solution)/shard_map/dot_general | solution.py:37
  156.1 5.1 multiply_convert_fusion.6
  174.9 5.7 fusion.15
  184.9 8.4 %fusion.3 = f32[1024,1152]{1,0:T(8,128)} fusion(bf16[2048,1024]{1,0:T(8,128)(2,1)S(1)} %copy-done.72, bf16[512,1152]{1,0:T(8,128)(2,1)S(1)} %get-tuple-element.171, bf16[512,1152]{1,0:T(8,128)(2,1)S(1)} %get-tuple-element.168, bf16[1024,1152]{1,0:T(8,128)(2,1)S(1)} %copy-done.105), kind=kOutput, calls=%fused_computation.6 | convolution fusion | flops 4845993984 | bytes 13631488 | tf_op jit(solution)/shard_map/dot_general | solution.py:41
  197.2 5.9 fusion.9
  234.8 13.9 %collective-permute-done.9 = f32[256,1024]{1,0:T(8,128)S(1)} collective-permute-done((f32[256,1024]{1,0:T(8,128)S(1)}, f32[256,1024]{1,0:T(8,128)S(1)}, u32[]{:S(2)}, u32[]{:S(2)}) %collective-permute-start.9) | collective-permute-done | bytes 1048608 | tf_op jit(solution)/shard_map/ppermute | solution.py:16
  258.8 12.4 %collective-permute-done.13 = f32[256,1024]{1,0:T(8,128)} collective-permute-done((f32[256,1024]{1,0:T(8,128)}, f32[256,1024]{1,0:T(8,128)}, u32[]{:S(2)}, u32[]{:S(2)}) %collective-permute-start.13) | collective-permute-done | bytes 1048608 | tf_op jit(solution)/shard_map/ppermute | solution.py:16
  277.3 5.8 constant_dynamic-update-slice_fusion.22
  283.6 10.0 %collective-permute-done.19 = f32[256,1024]{1,0:T(8,128)S(1)} collective-permute-done((f32[256,1024]{1,0:T(8,128)}, f32[256,1024]{1,0:T(8,128)S(1)}, u32[]{:S(2)}, u32[]{:S(2)}) %collective-permute-start.19) | collective-permute-done | bytes 1048608 | tf_op jit(solution)/shard_map/ppermute | solution.py:16
  293.7 22.3 %collective-permute-done.21 = f32[256,1024]{1,0:T(8,128)} collective-permute-done((f32[256,1024]{1,0:T(8,128)}, f32[256,1024]{1,0:T(8,128)}, u32[]{:S(2)}, u32[]{:S(2)}) %collective-permute-start.21) | collective-permute-done | bytes 1048608 | tf_op jit(solution)/shard_map/ppermute | solution.py:16
  327.6 48.4 %collective-permute-done.43 = f32[4,1,128,1152]{3,2,0,1:T(8,128)S(1)} collective-permute-done((f32[4,1,128,1152]{3,2,0,1:T(8,128)S(1)}, f32[4,1,128,1152]{3,2,0,1:T(8,128)S(1)}, u32[]{:S(2)}, u32[]{:S(2)}) %collective-permute-start.43) | collective-permute-done | bytes 2359328 | tf_op jit(solution)/shard_map/ppermute | solution.py:16
  377.9 21.9 %collective-permute-done.50 = f32[2,1,128,1152]{2,3,1,0:T(8,128)S(1)} collective-permute-done((f32[2,1,128,1152]{2,3,1,0:T(8,128)S(1)}, f32[2,1,128,1152]{2,3,1,0:T(8,128)S(1)}, u32[]{:S(2)}, u32[]{:S(2)}) %collective-permute-start.50) | collective-permute-done | bytes 1179680 | tf_op jit(solution)/shard_map/ppermute | solution.py:16
  404.4 34.5 %collective-permute-done.44 = f32[2,1,128,1152]{3,2,1,0:T(8,128)S(1)} collective-permute-done((f32[2,1,128,1152]{3,2,1,0:T(8,128)S(1)}, f32[2,1,128,1152]{3,2,1,0:T(8,128)S(1)}, u32[]{:S(2)}, u32[]{:S(2)}) %collective-permute-start.44) | collective-permute-done | bytes 1179680 | tf_op jit(solution)/shard_map/ppermute | solution.py:16
  448.2 18.1 %collective-permute-done.23 = f32[1024,256]{1,0:T(8,128)S(1)} collective-permute-done((f32[1024,256]{1,0:T(8,128)S(1)}, f32[1024,256]{1,0:T(8,128)S(1)}, u32[]{:S(2)}, u32[]{:S(2)}) %collective-permute-start.23) | collective-permute-done | bytes 1048608 | tf_op jit(solution)/shard_map/ppermute | solution.py:16
  483.7 8.0 %collective-permute-done.45 = f32[1,1,128,1152]{3,2,1,0:T(8,128)S(1)} collective-permute-done((f32[1,1,128,1152]{3,2,1,0:T(8,128)S(1)}, f32[1,1,128,1152]{3,2,1,0:T(8,128)S(1)}, u32[]{:S(2)}, u32[]{:S(2)}) %collective-permute-start.45) | collective-permute-done | bytes 589856 | tf_op jit(solution)/shard_map/ppermute | solution.py:16
  501.2 5.7 collective-permute-done.39
  507.2 17.1 %collective-permute-start.40 = (f32[2,1,128,512]{3,2,0,1:T(8,128)S(1)}, f32[2,1,128,512]{3,2,0,1:T(8,128)S(1)}, u32[]{:S(2)}, u32[]{:S(2)}) collective-permute-start(f32[2,1,128,512]{3,2,0,1:T(8,128)S(1)} %dynamic-slice_bitcast_fusion.7), channel_id=1, source_target_pairs={{0,8},{4,12},{8,0},{12,4},{16,24},{20,28},{24,16},{28,20},{1,9},{5... | collective-permute-start | bytes 1572872 | tf_op jit(solution)/shard_map/ppermute | solution.py:16
  531.0 5.2 collective-permute-done.40
  536.3 10.9 %collective-permute-done.27 = f32[512,1024]{1,0:T(8,128)S(1)} collective-permute-done((f32[512,1024]{1,0:T(8,128)S(1)}, f32[512,1024]{1,0:T(8,128)S(1)}, u32[]{:S(2)}, u32[]{:S(2)}) %collective-permute-start.27) | collective-permute-done | bytes 2097184 | tf_op jit(solution)/shard_map/ppermute | solution.py:16
  557.0 7.6 %collective-permute-start.41 = (f32[1,1,128,512]{3,2,0,1:T(8,128)S(1)}, f32[1,1,128,512]{3,2,0,1:T(8,128)S(1)}, u32[]{:S(2)}, u32[]{:S(2)}) collective-permute-start(f32[1,1,128,512]{3,2,0,1:T(8,128)S(1)} %constant_dynamic-slice_fusion.9), channel_id=1, source_target_pairs={{0,16},{4,20},{8,24},{12,28},{16,0},{20,4},{24,8},{28,12},{1,17},{... | collective-permute-start | bytes 786440 | tf_op jit(solution)/shard_map/ppermute | solution.py:16
  566.9 9.1 %collective-permute-done.41 = f32[1,1,128,512]{3,2,0,1:T(8,128)S(1)} collective-permute-done((f32[1,1,128,512]{3,2,0,1:T(8,128)S(1)}, f32[1,1,128,512]{3,2,0,1:T(8,128)S(1)}, u32[]{:S(2)}, u32[]{:S(2)}) %collective-permute-start.41) | collective-permute-done | bytes 262176 | tf_op jit(solution)/shard_map/ppermute | solution.py:16
  580.1 25.2 %collective-permute-done.42 = f32[128,256]{1,0:T(8,128)} collective-permute-done((f32[128,256]{1,0:T(8,128)S(1)}, f32[128,256]{1,0:T(8,128)}, u32[]{:S(2)}, u32[]{:S(2)}) %collective-permute-start.42) | collective-permute-done | bytes 131104 | tf_op jit(solution)/shard_map/ppermute | solution.py:16
  614.2 6.9 %collective-permute-start.38 = (f32[1,1,128,768]{3,2,1,0:T(8,128)S(1)}, f32[1,1,128,768]{3,2,1,0:T(8,128)S(1)}, u32[]{:S(2)}, u32[]{:S(2)}) collective-permute-start(f32[1,1,128,768]{3,2,1,0:T(8,128)S(1)} %constant_dynamic-slice_fusion.10), channel_id=1, source_target_pairs={{0,16},{4,20},{8,24},{12,28},{16,0},{20,4},{24,8},{28,12},{1,17},{... | collective-permute-start | bytes 1179656 | tf_op jit(solution)/shard_map/ppermute | solution.py:16
  625.3 6.7 %multiply_convert_fusion = bf16[2048,1024]{1,0:T(8,128)(2,1)} fusion(f32[2048,1024]{1,0:T(8,128)} %constant_dynamic-update-slice_fusion.19, f32[]{:T(128)S(6)} %add.452), kind=kLoop, calls=%fused_computation.5 | loop fusion | flops 4194304 | bytes 12582916 | tf_op jit(solution)/shard_map/convert_element_type | solution.py:29
  (453 shorter events, 236.5 us)
Async XLA Ops:
  11.6 26.4 %collective-permute-start.2 = (f32[256,1024]{1,0:T(8,128)}, f32[256,1024]{1,0:T(8,128)}, u32[]{:S(2)}, u32[]{:S(2)}) collective-permute-start(f32[256,1024]{1,0:T(8,128)} %convert_element_type.161), channel_id=1, source_target_pairs={{0,2},{1,3},{2,0},{3,1},{4,6},{5,7},{6,4},{7,5},{8,10},{9,11},{10,... | collective-permute-start | bytes 3145736 | tf_op jit(solution)/shard_map/ppermute | solution.py:16
  27.7 31.4 %collective-permute-start.1 = (f32[1024,256]{1,0:T(8,128)}, f32[1024,256]{1,0:T(8,128)}, u32[]{:S(2)}, u32[]{:S(2)}) collective-permute-start(f32[1024,256]{1,0:T(8,128)} %get-tuple-element.181), channel_id=1, source_target_pairs={{0,2},{1,3},{2,0},{3,1},{4,6},{5,7},{6,4},{7,5},{8,10},{9,11},{10,... | collective-permute-start | bytes 3145736 | tf_op jit(solution)/shard_map/ppermute | solution.py:16
  76.6 58.5 %collective-permute-start.4 = (f32[512,1024]{1,0:T(8,128)}, f32[512,1024]{1,0:T(8,128)}, u32[]{:S(2)}, u32[]{:S(2)}) collective-permute-start(f32[512,1024]{1,0:T(8,128)} %convert_element_type.164), channel_id=1, source_target_pairs={{0,1},{1,0},{2,3},{3,2},{4,5},{5,4},{6,7},{7,6},{8,9},{9,8},{10,11... | collective-permute-start | bytes 6291464 | tf_op jit(solution)/shard_map/ppermute | solution.py:16
  87.5 26.1 %collective-permute-start.6 = (f32[256,1024]{1,0:T(8,128)S(1)}, f32[256,1024]{1,0:T(8,128)S(1)}, u32[]{:S(2)}, u32[]{:S(2)}) collective-permute-start(f32[256,1024]{1,0:T(8,128)S(1)} %get-tuple-element.180), channel_id=1, source_target_pairs={{0,2},{1,3},{2,0},{3,1},{4,6},{5,7},{6,4},{7,5},{8,10},{9,11},{10,... | collective-permute-start | bytes 3145736 | tf_op jit(solution)/shard_map/ppermute | solution.py:16
  89.0 46.1 %collective-permute-start.10 = (f32[256,1024]{1,0:T(8,128)S(1)}, f32[256,1024]{1,0:T(8,128)S(1)}, u32[]{:S(2)}, u32[]{:S(2)}) collective-permute-start(f32[256,1024]{1,0:T(8,128)S(1)} %get-tuple-element.179), channel_id=1, source_target_pairs={{0,2},{1,3},{2,0},{3,1},{4,6},{5,7},{6,4},{7,5},{8,10},{9,11},{10,... | collective-permute-start | bytes 3145736 | tf_op jit(solution)/shard_map/ppermute | solution.py:16
  113.5 31.0 %collective-permute-start.7 = (f32[256,1024]{1,0:T(8,128)S(1)}, f32[256,1024]{1,0:T(8,128)S(1)}, u32[]{:S(2)}, u32[]{:S(2)}) collective-permute-start(f32[256,1024]{1,0:T(8,128)S(1)} %collective-permute-done.6), channel_id=1, source_target_pairs={{0,1},{1,0},{2,3},{3,2},{4,5},{5,4},{6,7},{7,6},{8,9},{9,8},{10,11... | collective-permute-start | bytes 3145736 | tf_op jit(solution)/shard_map/ppermute | solution.py:16
  135.1 31.8 %collective-permute-start.11 = (f32[256,1024]{1,0:T(8,128)S(1)}, f32[256,1024]{1,0:T(8,128)S(1)}, u32[]{:S(2)}, u32[]{:S(2)}) collective-permute-start(f32[256,1024]{1,0:T(8,128)S(1)} %collective-permute-done.10), channel_id=1, source_target_pairs={{0,1},{1,0},{2,3},{3,2},{4,5},{5,4},{6,7},{7,6},{8,9},{9,8},{10,11... | collective-permute-start | bytes 3145736 | tf_op jit(solution)/shard_map/ppermute | solution.py:16
  193.3 40.0 %collective-permute-start.5 = (f32[512,1024]{1,0:T(8,128)}, f32[512,1024]{1,0:T(8,128)}, u32[]{:S(2)}, u32[]{:S(2)}) collective-permute-start(f32[512,1024]{1,0:T(8,128)} %fusion.52), channel_id=1, source_target_pairs={{0,1},{1,0},{2,3},{3,2},{4,5},{5,4},{6,7},{7,6},{8,9},{9,8},{10,11... | collective-permute-start | bytes 6291464 | tf_op jit(solution)/shard_map/ppermute | solution.py:16
  193.8 28.9 %collective-permute-start.12 = (f32[256,1024]{1,0:T(8,128)}, f32[256,1024]{1,0:T(8,128)}, u32[]{:S(2)}, u32[]{:S(2)}) collective-permute-start(f32[256,1024]{1,0:T(8,128)} %fusion.97), channel_id=1, source_target_pairs={{0,1},{1,0},{2,3},{3,2},{4,5},{5,4},{6,7},{7,6},{8,9},{9,8},{10,11... | collective-permute-start | bytes 3145736 | tf_op jit(solution)/shard_map/ppermute | solution.py:16
  213.4 69.7 %collective-permute-start.17 = (f32[512,1024]{1,0:T(8,128)}, f32[512,1024]{1,0:T(8,128)}, u32[]{:S(2)}, u32[]{:S(2)}) collective-permute-start(f32[512,1024]{1,0:T(8,128)} %convolution_add_fusion.1), channel_id=1, source_target_pairs={{0,1},{1,0},{2,3},{3,2},{4,5},{5,4},{6,7},{7,6},{8,9},{9,8},{10,11... | collective-permute-start | bytes 6291464 | tf_op jit(solution)/shard_map/ppermute | solution.py:16
  227.5 95.7 %collective-permute-start.49 = (f32[2,2,128,1152]{2,3,1,0:T(8,128)}, f32[2,2,128,1152]{2,3,1,0:T(8,128)}, u32[]{:S(2)}, u32[]{:S(2)}) collective-permute-start(f32[2,2,128,1152]{2,3,1,0:T(8,128)} %bitcast.42), channel_id=1, source_target_pairs={{0,8},{4,12},{8,0},{12,4},{16,24},{20,28},{24,16},{28,20},{1,9},{5... | collective-permute-start | bytes 7077896 | tf_op jit(solution)/shard_map/ppermute | solution.py:16
  230.9 40.4 %collective-permute-start.13 = (f32[256,1024]{1,0:T(8,128)}, f32[256,1024]{1,0:T(8,128)}, u32[]{:S(2)}, u32[]{:S(2)}) collective-permute-start(f32[256,1024]{1,0:T(8,128)} %convolution_add_fusion.6), channel_id=1, source_target_pairs={{0,2},{1,3},{2,0},{3,1},{4,6},{5,7},{6,4},{7,5},{8,10},{9,11},{10,... | collective-permute-start | bytes 3145736 | tf_op jit(solution)/shard_map/ppermute | solution.py:16
  233.3 60.3 %collective-permute-start.19 = (f32[256,1024]{1,0:T(8,128)}, f32[256,1024]{1,0:T(8,128)S(1)}, u32[]{:S(2)}, u32[]{:S(2)}) collective-permute-start(f32[256,1024]{1,0:T(8,128)} %fusion.42), channel_id=1, source_target_pairs={{0,2},{1,3},{2,0},{3,1},{4,6},{5,7},{6,4},{7,5},{8,10},{9,11},{10,... | collective-permute-start | bytes 3145736 | tf_op jit(solution)/shard_map/ppermute | solution.py:16
  248.7 67.2 %collective-permute-start.21 = (f32[256,1024]{1,0:T(8,128)}, f32[256,1024]{1,0:T(8,128)}, u32[]{:S(2)}, u32[]{:S(2)}) collective-permute-start(f32[256,1024]{1,0:T(8,128)} %fusion.41), channel_id=1, source_target_pairs={{0,2},{1,3},{2,0},{3,1},{4,6},{5,7},{6,4},{7,5},{8,10},{9,11},{10,... | collective-permute-start | bytes 3145736 | tf_op jit(solution)/shard_map/ppermute | solution.py:16
  271.3 54.4 %collective-permute-start.46 = (f32[4,1,128,1152]{3,2,0,1:T(8,128)S(1)}, f32[4,1,128,1152]{3,2,0,1:T(8,128)S(1)}, u32[]{:S(2)}, u32[]{:S(2)}) collective-permute-start(f32[4,1,128,1152]{3,2,0,1:T(8,128)S(1)} %copy-done.31), channel_id=1, source_target_pairs={{0,4},{4,0},{8,12},{12,8},{16,20},{20,16},{24,28},{28,24},{1,5},{5... | collective-permute-start | bytes 7077896 | tf_op jit(solution)/shard_map/ppermute | solution.py:16
  283.1 92.9 %collective-permute-start.43 = (f32[4,1,128,1152]{3,2,0,1:T(8,128)S(1)}, f32[4,1,128,1152]{3,2,0,1:T(8,128)S(1)}, u32[]{:S(2)}, u32[]{:S(2)}) collective-permute-start(f32[4,1,128,1152]{3,2,0,1:T(8,128)S(1)} %copy-done.32), channel_id=1, source_target_pairs={{0,4},{4,0},{8,12},{12,8},{16,20},{20,16},{24,28},{28,24},{1,5},{5... | collective-permute-start | bytes 7077896 | tf_op jit(solution)/shard_map/ppermute | solution.py:16
  293.6 200.5 %collective-permute-start.14 = (f32[512,1024]{1,0:T(8,128)}, f32[512,1024]{1,0:T(8,128)S(1)}, u32[]{:S(2)}, u32[]{:S(2)}) collective-permute-start(f32[512,1024]{1,0:T(8,128)} %get-tuple-element.204), channel_id=1, source_target_pairs={{0,1},{1,0},{2,3},{3,2},{4,5},{5,4},{6,7},{7,6},{8,9},{9,8},{10,11... | collective-permute-start | bytes 6291464 | tf_op jit(solution)/shard_map/ppermute | solution.py:16
  315.9 178.2 %collective-permute-start.15 = (f32[512,1024]{1,0:T(8,128)}, f32[512,1024]{1,0:T(8,128)}, u32[]{:S(2)}, u32[]{:S(2)}) collective-permute-start(f32[512,1024]{1,0:T(8,128)} %get-tuple-element.204), channel_id=1, source_target_pairs={{0,2},{1,3},{2,0},{3,1},{4,6},{5,7},{6,4},{7,5},{8,10},{9,11},{10,... | collective-permute-start | bytes 6291464 | tf_op jit(solution)/shard_map/ppermute | solution.py:16
  323.2 117.6 %collective-permute-start.22 = (f32[512,1024]{1,0:T(8,128)S(1)}, f32[512,1024]{1,0:T(8,128)S(1)}, u32[]{:S(2)}, u32[]{:S(2)}) collective-permute-start(f32[512,1024]{1,0:T(8,128)S(1)} %get-tuple-element.158), channel_id=1, source_target_pairs={{0,1},{1,0},{2,3},{3,2},{4,5},{5,4},{6,7},{7,6},{8,9},{9,8},{10,11... | collective-permute-start | bytes 6291464 | tf_op jit(solution)/shard_map/ppermute | solution.py:16
  325.6 74.2 %collective-permute-start.50 = (f32[2,1,128,1152]{2,3,1,0:T(8,128)S(1)}, f32[2,1,128,1152]{2,3,1,0:T(8,128)S(1)}, u32[]{:S(2)}, u32[]{:S(2)}) collective-permute-start(f32[2,1,128,1152]{2,3,1,0:T(8,128)S(1)} %constant_dynamic-slice_fusion.3), channel_id=1, source_target_pairs={{0,4},{4,0},{8,12},{12,8},{16,20},{20,16},{24,28},{28,24},{1,5},{5... | collective-permute-start | bytes 3538952 | tf_op jit(solution)/shard_map/ppermute | solution.py:16
  399.8 39.1 %collective-permute-start.44 = (f32[2,1,128,1152]{3,2,1,0:T(8,128)S(1)}, f32[2,1,128,1152]{3,2,1,0:T(8,128)S(1)}, u32[]{:S(2)}, u32[]{:S(2)}) collective-permute-start(f32[2,1,128,1152]{3,2,1,0:T(8,128)S(1)} %dynamic-slice_bitcast_fusion.4), channel_id=1, source_target_pairs={{0,8},{4,12},{8,0},{12,4},{16,24},{20,28},{24,16},{28,20},{1,9},{5... | collective-permute-start | bytes 3538952 | tf_op jit(solution)/shard_map/ppermute | solution.py:16
  401.6 43.0 %collective-permute-start.51 = (f32[1,1,128,1152]{2,3,1,0:T(8,128)S(1)}, f32[1,1,128,1152]{2,3,1,0:T(8,128)S(1)}, u32[]{:S(2)}, u32[]{:S(2)}) collective-permute-start(f32[1,1,128,1152]{2,3,1,0:T(8,128)S(1)} %constant_dynamic-slice_fusion.2), channel_id=1, source_target_pairs={{0,16},{4,20},{8,24},{12,28},{16,0},{20,4},{24,8},{28,12},{1,17},{... | collective-permute-start | bytes 1769480 | tf_op jit(solution)/shard_map/ppermute | solution.py:16
  439.0 41.2 %collective-permute-start.48 = (f32[1,1,128,1152]{3,2,1,0:T(8,128)S(1)}, f32[1,1,128,1152]{3,2,1,0:T(8,128)S(1)}, u32[]{:S(2)}, u32[]{:S(2)}) collective-permute-start(f32[1,1,128,1152]{3,2,1,0:T(8,128)S(1)} %constant_dynamic-slice_fusion.6), channel_id=1, source_target_pairs={{0,16},{4,20},{8,24},{12,28},{16,0},{20,4},{24,8},{28,12},{1,17},{... | collective-permute-start | bytes 1769480 | tf_op jit(solution)/shard_map/ppermute | solution.py:16
  444.6 47.0 %collective-permute-start.45 = (f32[1,1,128,1152]{3,2,1,0:T(8,128)S(1)}, f32[1,1,128,1152]{3,2,1,0:T(8,128)S(1)}, u32[]{:S(2)}, u32[]{:S(2)}) collective-permute-start(f32[1,1,128,1152]{3,2,1,0:T(8,128)S(1)} %constant_dynamic-slice_fusion.7), channel_id=1, source_target_pairs={{0,16},{4,20},{8,24},{12,28},{16,0},{20,4},{24,8},{28,12},{1,17},{... | collective-permute-start | bytes 1769480 | tf_op jit(solution)/shard_map/ppermute | solution.py:16
  494.1 115.2 %collective-permute-start.16 = (f32[512,1024]{1,0:T(8,128)}, f32[512,1024]{1,0:T(8,128)}, u32[]{:S(2)}, u32[]{:S(2)}) collective-permute-start(f32[512,1024]{1,0:T(8,128)} %collective-permute-done.15), channel_id=1, source_target_pairs={{0,1},{1,0},{2,3},{3,2},{4,5},{5,4},{6,7},{7,6},{8,9},{9,8},{10,11... | collective-permute-start | bytes 6291464 | tf_op jit(solution)/shard_map/ppermute | solution.py:16
  498.1 38.2 %collective-permute-start.25 = (f32[512,1024]{1,0:T(8,128)}, f32[512,1024]{1,0:T(8,128)S(1)}, u32[]{:S(2)}, u32[]{:S(2)}) collective-permute-start(f32[512,1024]{1,0:T(8,128)} %fusion.67), channel_id=1, source_target_pairs={{0,1},{1,0},{2,3},{3,2},{4,5},{5,4},{6,7},{7,6},{8,9},{9,8},{10,11... | collective-permute-start | bytes 6291464 | tf_op jit(solution)/shard_map/ppermute | solution.py:16
  499.6 47.6 %collective-permute-start.27 = (f32[512,1024]{1,0:T(8,128)S(1)}, f32[512,1024]{1,0:T(8,128)S(1)}, u32[]{:S(2)}, u32[]{:S(2)}) collective-permute-start(f32[512,1024]{1,0:T(8,128)S(1)} %convolution_add_fusion), channel_id=1, source_target_pairs={{0,2},{1,3},{2,0},{3,1},{4,6},{5,7},{6,4},{7,5},{8,10},{9,11},{10,... | collective-permute-start | bytes 6291464 | tf_op jit(solution)/shard_map/ppermute | solution.py:16
  507.2 29.0 %collective-permute-start.40 = (f32[2,1,128,512]{3,2,0,1:T(8,128)S(1)}, f32[2,1,128,512]{3,2,0,1:T(8,128)S(1)}, u32[]{:S(2)}, u32[]{:S(2)}) collective-permute-start(f32[2,1,128,512]{3,2,0,1:T(8,128)S(1)} %dynamic-slice_bitcast_fusion.7), channel_id=1, source_target_pairs={{0,8},{4,12},{8,0},{12,4},{16,24},{20,28},{24,16},{28,20},{1,9},{5... | collective-permute-start | bytes 1572872 | tf_op jit(solution)/shard_map/ppermute | solution.py:16
  528.1 36.4 %collective-permute-start.36 = (f32[4,1,128,768]{3,2,0,1:T(8,128)S(1)}, f32[4,1,128,768]{3,2,0,1:T(8,128)S(1)}, u32[]{:S(2)}, u32[]{:S(2)}) collective-permute-start(f32[4,1,128,768]{3,2,0,1:T(8,128)S(1)} %dynamic-slice_bitcast_fusion.2), channel_id=1, source_target_pairs={{0,4},{4,0},{8,12},{12,8},{16,20},{20,16},{24,28},{28,24},{1,5},{5... | collective-permute-start | bytes 4718600 | tf_op jit(solution)/shard_map/ppermute | solution.py:16
  555.4 69.9 %collective-permute-start.29 = (f32[512,1024]{1,0:T(8,128)}, f32[512,1024]{1,0:T(8,128)}, u32[]{:S(2)}, u32[]{:S(2)}) collective-permute-start(f32[512,1024]{1,0:T(8,128)} %get-tuple-element.156), channel_id=1, source_target_pairs={{0,2},{1,3},{2,0},{3,1},{4,6},{5,7},{6,4},{7,5},{8,10},{9,11},{10,... | collective-permute-start | bytes 6291464 | tf_op jit(solution)/shard_map/ppermute | solution.py:16
  565.7 46.8 %collective-permute-start.37 = (f32[2,1,128,768]{3,2,1,0:T(8,128)}, f32[2,1,128,768]{3,2,1,0:T(8,128)S(1)}, u32[]{:S(2)}, u32[]{:S(2)}) collective-permute-start(f32[2,1,128,768]{3,2,1,0:T(8,128)} %dynamic-slice_bitcast_fusion.6), channel_id=1, source_target_pairs={{0,8},{4,12},{8,0},{12,4},{16,24},{20,28},{24,16},{28,20},{1,9},{5... | collective-permute-start | bytes 2359304 | tf_op jit(solution)/shard_map/ppermute | solution.py:16
  576.1 29.2 %collective-permute-start.42 = (f32[128,256]{1,0:T(8,128)S(1)}, f32[128,256]{1,0:T(8,128)}, u32[]{:S(2)}, u32[]{:S(2)}) collective-permute-start(f32[128,256]{1,0:T(8,128)S(1)} %slice.211), channel_id=1, source_target_pairs={{0,2},{1,3},{2,0},{3,1},{4,6},{5,7},{6,4},{7,5},{8,10},{9,11},{10,... | collective-permute-start | bytes 393224 | tf_op jit(solution)/shard_map/ppermute | solution.py:16
  (133 other events, 1554.6 us)

commit v2 on v1

v2 whole, which is shorter than its diff:
```python
import functools

import jax
import jax.numpy as jnp
from jax import lax
from jax.experimental import pallas as pl
from jax.experimental.pallas import tpu as pltpu
from jax.sharding import PartitionSpec as P

EPS = 1e-05


def shifted(block, axis, distance):
    devices = range(lax.axis_size(axis))
    route = [(i - distance, i) for i in devices if i - distance in devices]
    return lax.ppermute(block, axis, route)


def swap(block, axis, bit):
    return lax.ppermute(block, axis, [(i, i ^ bit) for i in range(lax.axis_size(axis))])


def swap_core(block):
    return swap(block, "tp", 1)


def swap_core_halves(block):
    size = block.shape[0] // 2
    return jnp.concatenate([swap_core(block[:size]), swap_core(block[size:])], axis=0)


class Clock:
    def __init__(self, value):
        self.value = value

    def passes(self, *values):
        values, self.value = lax.optimization_barrier((values, self.value))
        return values if len(values) > 1 else values[0]


def swap_y(block):
    return swap(block, "tp", 2)


def narrow(block):
    one = 1.0 + (lax.axis_index("tp") // lax.axis_size("tp")).astype(jnp.float32)
    return (block * one).astype(jnp.bfloat16)


def wide(block):
    return block.astype(jnp.float32)


def dot(left, right):
    return jnp.dot(left, right, preferred_element_type=jnp.float32)


def inner_rows(left, right):
    return lax.dot_general(
        left, right, (((0,), (0,)), ((), ())), preferred_element_type=jnp.float32
    )


def times_back(left, right):
    return lax.dot_general(
        left, right, (((1,), (1,)), ((), ())), preferred_element_type=jnp.float32
    )


def adamw(weight, grad, mean, square, decay, rate):
    mean_new = 0.9 * mean + 0.1 * grad
    square_new = 0.95 * square + 0.05 * grad * grad
    mean_hat = mean_new / (1.0 - 0.9**3)
    square_hat = square_new / (1.0 - 0.95**3)
    weight_new = weight - rate * (mean_hat / (jnp.sqrt(square_hat) + 1e-08) + decay * weight)
    return (weight_new, mean_new, square_new)


def norm_back(dnormed, normed, inverse):
    return inverse * (dnormed - normed * jnp.mean(dnormed * normed, axis=-1, keepdims=True))


def log_two(number):
    bits = number.bit_length() - 1
    assert number == 1 << bits
    return bits


def ffn_kernel(count, place, *refs):
    pieces, (cotangent, *weights) = refs[:count], refs[count : count + 4]
    outs, scratch = refs[-15:-7], refs[-7:]
    htwo_out, act_out, dgate_out, dup_out, fkeep, fsend, dkeep, dsend = outs
    w_gate, w_up, w_down, cots, htwo, weight_sems, cot_sems = scratch
    step = pl.program_id(0)
    size = htwo.shape[0]
    copies = [
        pltpu.make_async_copy(source, target, weight_sems.at[k])
        for k, (source, target) in enumerate(zip(weights, (w_gate, w_up, w_down)))
    ]

    def cot_copy(index):
        rows = pl.ds(pl.multiple_of(place[index] * size, size), size)
        slot = index % 2
        return pltpu.make_async_copy(cotangent.at[rows], cots.at[slot], cot_sems.at[slot])

    @pl.when(step == 0)
    def _():
        copies[0].start()
        copies[1].start()
        cot_copy(0).start()
        copies[2].start()

    @pl.when(step + 1 < count)
    def _():
        cot_copy(step + 1).start()

    for k, ref in enumerate(pieces):

        @pl.when(step == k)
        def _(ref=ref):
            htwo[...] = ref[...].astype(jnp.bfloat16)

    htwo_out[...] = htwo[...]

    @pl.when(step == 0)
    def _():
        copies[0].wait()

    gate = dot(htwo[...], w_gate[...])

    @pl.when(step == 0)
    def _():
        copies[1].wait()

    upval = dot(htwo[...], w_up[...])
    cot_copy(step).wait()

    @pl.when(step == 0)
    def _():
        copies[2].wait()

    dact = times_back(cots[step % 2], w_down[...])
    sigma = jax.nn.sigmoid(gate)
    silu_gate = gate * sigma
    act = (silu_gate * upval).astype(jnp.bfloat16)
    dgate = (dact * upval * (sigma * (1.0 + gate * (1.0 - sigma)))).astype(jnp.bfloat16)
    dup = (dact * silu_gate).astype(jnp.bfloat16)
    act_out[...] = act
    dgate_out[...] = dgate
    dup_out[...] = dup
    dhtwo = times_back(dgate, w_gate[...]) + times_back(dup, w_up[...])
    ffn = dot(act, w_down[...])

    @pl.when(step % 2 == 0)
    def _():
        fkeep[...] = ffn
        dkeep[...] = dhtwo

    @pl.when(step % 2 == 1)
    def _():
        fsend[...] = ffn
        dsend[...] = dhtwo


def feed_forward(place, pieces, cotangent, weights, kept):
    features = cotangent.shape[1]
    size = pieces[0].shape[0]
    units = weights[0].shape[1]
    whole = lambda ref: pl.BlockSpec(ref.shape, lambda i, p: (0, 0), pipeline_mode=pl.Buffered(1))
    spot = lambda width: pl.BlockSpec((size, width), lambda i, p: (p[i], 0))
    part = pl.BlockSpec((size, features), lambda i, p: (i // 2, 0))
    kept = [] if kept is None else list(kept)
    shapes = [
        pltpu.HBM((cotangent.shape[0], width), jnp.bfloat16)
        for width in (features, units, units, units)
    ]
    shapes += [pltpu.HBM((size * len(pieces) // 2, features), jnp.float32)] * 4
    return pl.pallas_call(
        functools.partial(ffn_kernel, len(pieces)),
        grid_spec=pltpu.PrefetchScalarGridSpec(
            num_scalar_prefetch=1,
            grid=(len(pieces),),
            in_specs=[whole(ref) for ref in pieces]
            + [pl.BlockSpec(memory_space=pltpu.HBM)] * 4
            + [pl.BlockSpec(memory_space=pl.ANY)] * len(kept),
            out_specs=[spot(features), spot(units), spot(units), spot(units)] + [part] * 4,
            scratch_shapes=[pltpu.VMEM(w.shape, w.dtype) for w in weights]
            + [
                pltpu.VMEM((2, size, features), cotangent.dtype),
                pltpu.VMEM((size, features), jnp.bfloat16),
                pltpu.SemaphoreType.DMA((3,)),
                pltpu.SemaphoreType.DMA((2,)),
            ],
        ),
        out_shape=shapes,
        input_output_aliases={5 + len(pieces) + i: i for i in range(len(kept))},
        compiler_params=pltpu.CompilerParams(vmem_limit_bytes=57 * 2**20),
        cost_estimate=pl.CostEstimate(flops=3 * 10**10, bytes_accessed=10**7, transcendentals=0),
    )(jnp.stack(place).astype(jnp.int32), *pieces, cotangent, *weights, *kept)


def place_kernel(pieces, spots, *refs):
    out = refs[-1]
    size = out.shape[0]
    for step, (index, part) in enumerate(pieces):

        @pl.when(pl.program_id(0) == step)
        def _(step=step, index=index, part=part):
            out[...] = refs[index][part * size : (part + 1) * size, :].astype(out.dtype)


def place_rows(blocks, spots, size, count, dtype, whole=None):
    width = blocks[0].shape[1]
    held = [] if whole is None else [whole]
    pieces = [(k, i) for k, block in enumerate(blocks) for i in range(block.shape[0] // size)]
    return pl.pallas_call(
        functools.partial(place_kernel, pieces),
        grid_spec=pltpu.PrefetchScalarGridSpec(
            num_scalar_prefetch=1,
            grid=(len(pieces),),
            in_specs=[
                pl.BlockSpec(block.shape, lambda i, p: (0, 0), pipeline_mode=pl.Buffered(1))
                for block in blocks
            ]
            + [pl.BlockSpec(memory_space=pl.ANY)] * len(held),
            out_specs=pl.BlockSpec((size, width), lambda i, p: (p[i], 0)),
        ),
        out_shape=jax.ShapeDtypeStruct((count, width), dtype),
        input_output_aliases={1 + len(blocks): 0} if held else {},
        compiler_params=pltpu.CompilerParams(vmem_limit_bytes=32 * 2**20),
        cost_estimate=pl.CostEstimate(
            flops=0, bytes_accessed=8 * len(pieces) * size * width, transcendentals=0
        ),
    )(jnp.stack(spots).astype(jnp.int32), *blocks, *held)


def sum_kernel(wide_rows, parts, picks, *refs):
    right, send, keep = refs[parts], refs[-2], refs[-1]
    left = jnp.concatenate([ref[...] for ref in refs[:parts]], axis=1)
    total = inner_rows(left, right[...])

    @pl.when(pl.program_id(0) == 0)
    def _():
        send[...] = total

    @pl.when(pl.program_id(0) == 1)
    def _():
        keep[...] = total


def sum_halves(left, right, place, bit):
    shards = lax.axis_size("seq")
    width = left.shape[1] // shards
    parts = shards // 2
    mine = (place >> bit) & 1
    low = jnp.arange(parts, dtype=jnp.int32)
    low, high = low & ((1 << bit) - 1), low >> bit
    base = (high << (bit + 1)) | low
    picks = jnp.concatenate([base | ((1 - mine) << bit), base | (mine << bit)]).astype(jnp.int32)
    if width % 128 != 0:
        total = inner_rows(left, right).reshape(-1, 2, 1 << bit, width * right.shape[1])
        return tuple(
            lax.dynamic_index_in_dim(total, which, 1, keepdims=False).reshape(-1, right.shape[1])
            for which in (1 - mine, mine)
        )
    count, units = right.shape
    half = jax.ShapeDtypeStruct((parts * width, units), jnp.float32)
    pick = lambda k: pl.BlockSpec((count, width), lambda i, p, k=k: (0, p[i * parts + k]))
    fixed = lambda shape: pl.BlockSpec(shape, lambda i, p: (0, 0), pipeline_mode=pl.Buffered(1))
    return pl.pallas_call(
        functools.partial(sum_kernel, width, parts),
        grid_spec=pltpu.PrefetchScalarGridSpec(
            num_scalar_prefetch=1,
            grid=(2,),
            in_specs=[pick(k) for k in range(parts)] + [fixed(right.shape)],
            out_specs=[fixed(half.shape)] * 2,
        ),
        out_shape=[pltpu.HBM(half.shape, half.dtype)] * 2,
        compiler_params=pltpu.CompilerParams(vmem_limit_bytes=57 * 2**20),
        cost_estimate=pl.CostEstimate(flops=10**12, bytes_accessed=10**7, transcendentals=0),
    )(picks, *[left] * parts, right)


def step_kernel(picks, *refs):
    keep_one, came_one, keep_two, came_two, send, keep = refs
    send[...] = keep_one[...] + came_one[...]
    keep[...] = keep_two[...] + came_two[...]


def halve_sum(kept, came, mine, low):
    blocks, width, units = kept.shape
    if width % 8 != 0 or units % 128 != 0:
        pairs = (kept + came).reshape(-1, 2, low, width, units)
        return tuple(
            lax.dynamic_index_in_dim(pairs, which, 1, keepdims=False).reshape(-1, width, units)
            for which in (1 - mine, mine)
        )
    index = jnp.arange(blocks // 2, dtype=jnp.int32)
    base = (index // low) * (2 * low) + index % low
    picks = jnp.concatenate([base + (1 - mine) * low, base + mine * low]).astype(jnp.int32)
    one = pl.BlockSpec((1, width, units), lambda i, p: (p[i], 0, 0))
    two = pl.BlockSpec((1, width, units), lambda i, p: (p[i + blocks // 2], 0, 0))
    half = pl.BlockSpec((1, width, units), lambda i, p: (i, 0, 0))
    return pl.pallas_call(
        step_kernel,
        grid_spec=pltpu.PrefetchScalarGridSpec(
            num_scalar_prefetch=1,
            grid=(blocks // 2,),
            in_specs=[one, one, two, two],
            out_specs=[half, half],
        ),
        out_shape=[jax.ShapeDtypeStruct((blocks // 2, width, units), kept.dtype)] * 2,
        cost_estimate=pl.CostEstimate(flops=10**12, bytes_accessed=10**7, transcendentals=0),
    )(picks, kept, came, kept, came)


class Halving:
    def __init__(self, clock, left, right, place, order):
        shards = lax.axis_size("seq")
        self.shape = (left.shape[1] // shards, right.shape[1])
        self.place = place
        self.order = list(order)
        self.left = list(range(log_two(shards)))
        left, right = clock.passes(left, right)
        send, keep = clock.passes(*sum_halves(left, right, place, order[0]))
        self.send, self.keep = send.reshape((-1,) + self.shape), keep.reshape((-1,) + self.shape)

    def start(self, clock=None):
        bit = self.order.pop(0)
        self.left.remove(bit)
        send = self.send if clock is None else clock.passes(self.send)
        self.came = swap(send, "seq", 1 << bit)

    def finish(self, clock):
        came = clock.passes(self.came)
        if not self.order:
            self.total = self.keep + came
            return
        bit = self.order[0]
        low = 1 << self.left.index(bit)
        self.send, self.keep = halve_sum(self.keep, came, (self.place >> bit) & 1, low)

    def final(self, clock):
        self.finish(clock)
        while self.order:
            self.start()
            self.finish(clock)
        return self.total[0]


def sum_all(block, axis):
    for bit in range(log_two(lax.axis_size(axis))):
        block = block + swap(block, axis, 1 << bit)
    return block


def body(
    tokens,
    cotangent,
    start_flags,
    gain_mixer,
    w_bgate,
    w_cgate,
    w_input,
    conv_kernel,
    w_output,
    gain_ffn,
    w_gate,
    w_up,
    w_down,
    mean_gain_mixer,
    square_gain_mixer,
    mean_w_bgate,
    square_w_bgate,
    mean_w_cgate,
    square_w_cgate,
    mean_w_input,
    square_w_input,
    mean_conv_kernel,
    square_conv_kernel,
    mean_w_output,
    square_w_output,
    mean_gain_ffn,
    square_gain_ffn,
    mean_w_gate,
    square_w_gate,
    mean_w_up,
    square_w_up,
    mean_w_down,
    square_w_down,
):
    count, features = tokens.shape
    half = count // 2
    part = count // 4
    sub = count // 8
    place = lax.axis_index("seq")
    rank = lax.axis_index("tp")
    upper = rank // 2
    core = rank % 2
    near_first = list(range(log_two(lax.axis_size("seq"))))
    far_first = [near_first[1], near_first[0]] + near_first[2:]
    quarter = w_output.shape[0]

    def rows(block, index, size):
        return lax.dynamic_slice_in_dim(block, index * size, size, 0)

    def piece(chip, j, which):
        return chip * 4 + j * 2 + which

    def joined(mine, other):
        return jnp.where(
            core == 0,
            jnp.concatenate([mine, other], axis=0),
            jnp.concatenate([other, mine], axis=0),
        )

    clock = Clock(gain_mixer)
    w_output_far = narrow(swap_y(wide(w_output)))
    w_output_both = jnp.concatenate([w_output, w_output_far], axis=0)
    xin = tokens.astype(jnp.float32)
    inverse_one = lax.rsqrt(jnp.mean(xin * xin, axis=-1, keepdims=True) + EPS)
    norm_one = xin * inverse_one
    hone = (norm_one * gain_mixer).astype(jnp.bfloat16)
    last = hone[-8:]
    mixed_last = dot(last, w_bgate) * dot(last, w_input)
    cgate_next = shifted(dot(hone[:8], w_cgate), "seq", -1)
    keeper = (1 - start_flags[0]).astype(jnp.float32)
    kernel = conv_kernel.astype(jnp.float32)
    previous = shifted(mixed_last, "seq", 1)[-2:] * keeper
    bgate = dot(hone, w_bgate)
    cgate = dot(hone, w_cgate)
    xval = dot(hone, w_input)
    mixed_in = bgate * xval
    extended = jnp.concatenate([previous, mixed_in], axis=0)
    conv = kernel[2] * mixed_in + kernel[1] * extended[1:-1] + kernel[0] * extended[:-2]
    gated = (cgate * conv).astype(jnp.bfloat16)

    gated_both, resid, norm_two, inverse_two, htwo_own, htwo_near = [], [], [], [], [], []
    htwo_across = []
    w_all = jnp.concatenate([w_bgate, w_cgate, w_input], axis=1)
    x_own = [
        rows(tokens, piece(upper, j, core), sub).astype(jnp.float32) for j in range(2)
    ]
    inverse_own = [
        lax.rsqrt(jnp.mean(x * x, axis=-1, keepdims=True) + EPS) for x in x_own
    ]
    far = swap_y(wide(rows(gated, 1 - upper, half)))
    w_all = jnp.concatenate([w_all, narrow(swap_core(wide(w_all)))], axis=1)
    w_all, inverse_own, w_output_far, w_output_both, cgate_next = clock.passes(
        w_all, inverse_own, w_output_far, w_output_both, cgate_next
    )
    far = clock.passes(far)
    fars = [far[:part], far[part:]]
    for j in range(2):
        both = jnp.concatenate([rows(gated, upper * 2 + j, part), narrow(fars[j])], axis=1)
        gated_both.append(both)
        mix_send = dot(rows(both, 1 - core, sub), w_output_both)
        mix_keep = dot(rows(both, core, sub), w_output_both)
        resid.append(x_own[j] + (mix_keep + swap_core(mix_send)))
        inverse_two.append(
            lax.rsqrt(jnp.mean(resid[j] * resid[j], axis=-1, keepdims=True) + EPS)
        )
        norm_two.append(resid[j] * inverse_two[j])
        htwo_own.append(wide((norm_two[j] * gain_ffn).astype(jnp.bfloat16)))
        htwo_across.append(swap_y(htwo_own[j]))
        htwo_near.append(swap_core(htwo_own[j]))

    weights = (w_gate, w_up, w_down)
    spots = [piece(upper, j, which) for j in range(2) for which in (core, 1 - core)]
    pieces = [v for j in range(2) for v in (htwo_own[j], htwo_near[j])]
    outs = clock.passes(*feed_forward(spots, pieces, cotangent, weights, None))
    kept, ffn_here, dhtwo_here = outs[:4], outs[4:6], outs[6:]
    ffn_there, dhtwo_across = [], []
    dhtwo_here = dhtwo_here[0] + swap_core(dhtwo_here[1])
    for j in range(2):
        if j == 1:
            dhtwo_here = clock.passes(dhtwo_here)
        across = clock.passes(htwo_across[j])
        spots = [piece(1 - upper, j, which) for which in (core, 1 - core)]
        pieces = [across, swap_core(across)]
        outs = clock.passes(*feed_forward(spots, pieces, cotangent, weights, kept))
        kept = outs[:4]
        ffn_there.append(outs[4:6])
        dhtwo_across.append(swap_y(clock.passes(outs[6] + swap_core_halves(outs[7]))))
    htwo_all, act_all, dgate_all, dup_all = kept
    def to_previous(block, chip):
        ranks = lax.axis_size("tp")
        route = [
            (s * ranks + c, (s - 1) * ranks + 2 * chip + c)
            for s in range(1, lax.axis_size("seq"))
            for c in range(2)
        ]
        return lax.ppermute(block, ("seq", "tp"), route)

    dresid, dgain_ffn, dmix, dgated_near, dgated_far = [], 0.0, [], [], []

    def before_swap(j):
        gout = rows(cotangent, piece(upper, j, core), sub).astype(jnp.float32)
        dhtwo = dhtwo_here[j * sub : (j + 1) * sub] + clock.passes(dhtwo_across[j])
        dresid.append(gout + norm_back(dhtwo * gain_ffn, norm_two[j], inverse_two[j]))
        dmix_own = clock.passes(wide(dresid[j].astype(jnp.bfloat16)))
        return dmix_own, swap_core(dmix_own), jnp.sum(dhtwo * norm_two[j], axis=0)

    def after_swap(dmix_own, came):
        dmix.append(narrow(joined(dmix_own, clock.passes(came))))
        near, far = clock.passes(
            times_back(dmix[-1], w_output), times_back(dmix[-1], w_output_far)
        )
        dgated_near.append(near)
        dgated_far.append(swap_y(far))
        return near, far

    def ffn_sum(j):
        keep, send = clock.passes(*ffn_there[j])
        return keep + swap_core(send)

    dmix_own, came, gain_part = before_swap(0)
    dgain_ffn = dgain_ffn + gain_part
    down = Halving(clock, cotangent, act_all, place, far_first)
    near, far = after_swap(dmix_own, came)
    dgated_next = to_previous(near[:8] * keeper, 0) + to_previous(far[:8] * keeper, 1)
    gate = Halving(clock, htwo_all, dgate_all, place, near_first)
    down.start(clock)
    gate.start(clock)
    dgated_next = clock.passes(dgated_next)
    dmix_own, came, gain_part = before_swap(1)
    dgain_ffn = dgain_ffn + gain_part
    dgated_far[0] = clock.passes(dgated_far[0])
    ffn_far = [ffn_sum(j) for j in range(2)]
    upw = Halving(clock, htwo_all, dup_all, place, near_first)
    after_swap(dmix_own, came)
    ffn_across = [swap_y(clock.passes(block)) for block in ffn_far]
    outw = Halving(
        clock,
        jnp.concatenate(dmix, axis=0),
        jnp.concatenate(gated_both, axis=0),
        place,
        near_first,
    )
    dgated_far[1] = clock.passes(dgated_far[1])
    dgated = jnp.where(
        upper == 0,
        jnp.concatenate(dgated_near + dgated_far, axis=0),
        jnp.concatenate(dgated_far + dgated_near, axis=0),
    )

    dcgate = (dgated * conv).astype(jnp.bfloat16)
    dconv = dgated * cgate
    dkernel = jnp.stack(
        [
            jnp.sum(dconv * extended[:-2], axis=0),
            jnp.sum(dconv * extended[1:-1], axis=0),
            jnp.sum(dconv * mixed_in, axis=0),
        ],
        axis=0,
    )
    dextended = (
        jnp.pad(kernel[2] * dconv, ((2, 0), (0, 0)))
        + jnp.pad(kernel[1] * dconv, ((1, 1), (0, 0)))
        + jnp.pad(kernel[0] * dconv, ((0, 2), (0, 0)))
    )
    dconv_next = dgated_next[:2] * cgate_next[:2]
    returned = jnp.concatenate(
        [kernel[0] * dconv_next[:1], kernel[1] * dconv_next[:1] + kernel[0] * dconv_next[1:]],
        axis=0,
    )
    dmixed = dextended[2:] + jnp.pad(returned, ((count - 2, 0), (0, 0)))
    dbgate = (dmixed * xval).astype(jnp.bfloat16)
    dxval = (dmixed * bgate).astype(jnp.bfloat16)
    dall = jnp.concatenate([dbgate, dcgate, dxval], axis=1)
    by_core = dall.reshape(4, 2, sub, dall.shape[1])
    send = lax.dynamic_index_in_dim(by_core, 1 - core, 1, keepdims=False)
    came = swap_core(clock.passes(wide(send)))
    down.finish(clock)
    gate.finish(clock)
    upw.start(clock)
    gate.start(clock)
    inw = Halving(clock, hone, dall, place, near_first)
    came = clock.passes(came)
    ffn_here = clock.passes(*ffn_here)
    ffn_near = swap_core(ffn_here[1])
    dall_own = lax.dynamic_index_in_dim(by_core, core, 1, keepdims=False)
    dall_own = jnp.concatenate([dall_own, narrow(came)], axis=2)

    def back_rows(chip, j):
        block = lax.dynamic_index_in_dim(dall_own, chip * 2 + j, 0, keepdims=False)
        return times_back(block, w_all)

    dhone_across = [swap_y(clock.passes(back_rows(1 - upper, j))) for j in range(2)]
    dhone_near = [back_rows(upper, j) for j in range(2)]

    ffn_across[0] = clock.passes(ffn_across[0])
    gate.finish(clock)
    gate.start(clock)
    ffn_near = ffn_here[0] + clock.passes(ffn_near)
    dgain_mixer, grads_own, grads_across = 0.0, [], []

    def arrives(j):
        norm_own = x_own[j] * inverse_own[j]
        dhone = dhone_near[j] + clock.passes(dhone_across[j])
        grad_own = dresid[j] + norm_back(dhone * gain_mixer, norm_own, inverse_own[j])
        grads_own.append(grad_own)
        return jnp.sum(dhone * norm_own, axis=0)

    ffn_across[1] = clock.passes(ffn_across[1])
    ffn = ffn_near + jnp.concatenate(ffn_across, axis=0)
    block_own = wide((jnp.concatenate(resid, axis=0) + ffn).astype(jnp.bfloat16))
    dgain_mixer = dgain_mixer + arrives(0)
    grads_across.append(swap_y(clock.passes(grads_own[0])))
    upw.finish(clock)
    inw.start(clock)
    upw.start(clock)
    dgain_mixer = dgain_mixer + arrives(1)
    grads_across.append(swap_y(clock.passes(grads_own[1])))
    grads_near = swap_core(jnp.concatenate(grads_own, axis=0))
    gains = jnp.concatenate([dgain_mixer, dgain_ffn]).reshape(-1, 128)
    small = jnp.concatenate([gains, dkernel.reshape(-1, 128)], axis=0)
    grad_gate = gate.final(clock)
    upw.finish(clock)
    upw.start(clock)
    grads_near = clock.passes(grads_near)
    grads_across[0] = clock.passes(grads_across[0])
    block_across = [swap_y(clock.passes(block_own[:sub]))]
    inw.finish(clock)
    down.start(clock)
    inw.start(clock)
    seq_bits = range(log_two(lax.axis_size("seq")))
    small = clock.passes(small)
    small_came = swap(small, "seq", 1)
    grad_upw = upw.final(clock)
    grads_across[1] = clock.passes(grads_across[1])
    block_across.append(swap_y(clock.passes(block_own[sub:])))
    inw.finish(clock)
    inw.start(clock)
    for bit in seq_bits:
        small = small + clock.passes(small_came)
        if bit + 1 < len(seq_bits):
            small_came = swap(small, "seq", 2 << bit)
        if bit == 0:
            down.finish(clock)
            outw.start(clock)
            down.start(clock)
    grads_corner = swap_core(jnp.concatenate(grads_across, axis=0))
    grad_in = inw.final(clock)
    block_across[0] = clock.passes(block_across[0])
    outw.finish(clock)
    outw.start(clock)
    gains = sum_all(small[: gains.shape[0]], "tp").reshape(2, features)
    dkernel = small[gains.size // 128 :].reshape(dkernel.shape)
    grad_down = down.final(clock)
    block_near = swap_core(clock.passes(block_own))
    grad_tokens = place_rows(
        [*grads_own, grads_near, *grads_across, clock.passes(grads_corner)],
        [piece(k, j, w) for k in (upper, 1 - upper) for w in (core, 1 - core) for j in range(2)],
        sub,
        count,
        jnp.float32,
    )
    outw.finish(clock)
    outw.start(clock)
    block_near = clock.passes(block_near)
    block_across[1] = clock.passes(block_across[1])
    block_corner = swap_core(jnp.concatenate(block_across, axis=0))
    grad_outw_both = outw.final(clock)
    grad_outw = grad_outw_both[:, :quarter] + swap_y(grad_outw_both[:, quarter:])
    grad_outw = lax.optimization_barrier(grad_outw.T)
    grad_down = lax.optimization_barrier(grad_down.T)
    block_out = place_rows(
        [block_own, block_near, *block_across, block_corner],
        [piece(k, j, w) for k in (upper, 1 - upper) for w in (core, 1 - core) for j in range(2)],
        sub,
        count,
        jnp.bfloat16,
    )

    width = features // lax.axis_size("seq")

    def rows_of(weight):
        return lax.dynamic_slice_in_dim(weight, place * width, width, 0).astype(jnp.float32)

    def columns_of(weight):
        return lax.dynamic_slice_in_dim(weight, place * width, width, 1).astype(jnp.float32)

    params = [
        clock.value,
        rows_of(w_bgate),
        rows_of(w_cgate),
        rows_of(w_input),
        kernel,
        columns_of(w_output),
        gain_ffn,
        rows_of(w_gate),
        rows_of(w_up),
        columns_of(w_down),
    ]
    grads = [
        gains[0],
        grad_in[:, :quarter],
        grad_in[:, quarter : 2 * quarter],
        grad_in[:, 2 * quarter :],
        dkernel,
        grad_outw,
        gains[1],
        grad_gate,
        grad_upw,
        grad_down,
    ]
    moments = [
        (mean_gain_mixer, square_gain_mixer),
        (mean_w_bgate, square_w_bgate),
        (mean_w_cgate, square_w_cgate),
        (mean_w_input, square_w_input),
        (mean_conv_kernel, square_conv_kernel),
        (mean_w_output, square_w_output),
        (mean_gain_ffn, square_gain_ffn),
        (mean_w_gate, square_w_gate),
        (mean_w_up, square_w_up),
        (mean_w_down, square_w_down),
    ]
    decays = [0.0, 0.1, 0.1, 0.1, 0.1, 0.1, 0.0, 0.1, 0.1, 0.1]
    rates = [0.2, 0.01, 0.01, 0.01, 0.2, 0.01, 0.2, 0.01, 0.01, 0.01]
    outs = [block_out, grad_tokens]
    for index in range(10):
        weight_new, mean_new, square_new = adamw(
            params[index],
            grads[index],
            moments[index][0],
            moments[index][1],
            decays[index],
            rates[index],
        )
        outs = outs + [grads[index], weight_new, mean_new, square_new]
    return tuple(outs)


def solution(mesh):
    in_specs = (
        P("seq", None),
        P("seq", None),
        P("seq"),
        P(),
        P(None, "tp"),
        P(None, "tp"),
        P(None, "tp"),
        P(None, "tp"),
        P("tp", None),
        P(),
        P(None, "tp"),
        P(None, "tp"),
        P("tp", None),
        P(),
        P(),
        P("seq", "tp"),
        P("seq", "tp"),
        P("seq", "tp"),
        P("seq", "tp"),
        P("seq", "tp"),
        P("seq", "tp"),
        P(None, "tp"),
        P(None, "tp"),
        P("tp", "seq"),
        P("tp", "seq"),
        P(),
        P(),
        P("seq", "tp"),
        P("seq", "tp"),
        P("seq", "tp"),
        P("seq", "tp"),
        P("tp", "seq"),
        P("tp", "seq"),
    )
    out_specs = (
        P("seq", None),
        P("seq", None),
        P(),
        P(),
        P(),
        P(),
        P("seq", "tp"),
        P("seq", "tp"),
        P("seq", "tp"),
        P("seq", "tp"),
        P("seq", "tp"),
        P("seq", "tp"),
        P("seq", "tp"),
        P("seq", "tp"),
        P("seq", "tp"),
        P("seq", "tp"),
        P("seq", "tp"),
        P("seq", "tp"),
        P(None, "tp"),
        P(None, "tp"),
        P(None, "tp"),
        P(None, "tp"),
        P("tp", "seq"),
        P("tp", "seq"),
        P("tp", "seq"),
        P("tp", "seq"),
        P(),
        P(),
        P(),
        P(),
        P("seq", "tp"),
        P("seq", "tp"),
        P("seq", "tp"),
        P("seq", "tp"),
        P("seq", "tp"),
        P("seq", "tp"),
        P("seq", "tp"),
        P("seq", "tp"),
        P("tp", "seq"),
        P("tp", "seq"),
        P("tp", "seq"),
        P("tp", "seq"),
    )
    return jax.shard_map(body, mesh=mesh, in_specs=in_specs, out_specs=out_specs, check_vma=False)
```

time: 662 us -> 525 us (0.79)
  waiting for transfers between devices: 323 us -> 110 us
  Pallas kernels: 0 us -> 168 us
  matrix products: 133 us -> 33.5 us
  other arithmetic: 49.6 us -> 104 us
  starting transfers between devices: 84.1 us -> 59.2 us
  local copies, waits for them, and re-layouts: 59.2 us -> 39.9 us
    ppermute x50 -> x59, waiting for transfers between devices: 320 us -> 110 us  [swap(): lax.ppermute(block, axis, [(i, i ^ bit) for i in range(lax.axis_size(axis...]
    pallas_call x0 -> x20, Pallas kernels: none -> 168 us  [the longest x3 64.1 us: feed_forward(): pl.pallas_call(functools.partial(ffn_kernel, len(pieces)), grid_spec=pltp...]
    dot_general x19 -> x10, matrix products: 62.2 us -> 18.9 us  [dot(): return jnp.dot(left, right, preferred_element_type=jnp.float32)]
    dot_general x21 -> x8, matrix products: 46 us -> 14.7 us  [times_back(): lax.dot_general(left, right, (((1,), (1,)), ((), ())), preferred_element_...]
    ppermute x50 -> x59, starting transfers between devices: 77.7 us -> 51.2 us  [swap(): lax.ppermute(block, axis, [(i, i ^ bit) for i in range(lax.axis_size(axis...]
    dot_general x5 -> x0, matrix products: 25 us -> none  [inner_rows(): lax.dot_general(left, right, (((0,), (0,)), ((), ())), preferred_element_...]
    concatenate x2 -> x12, other arithmetic: 0.95 us -> 18.6 us  [the longest x1 3.26 us: body(): grads_near = swap_core(jnp.concatenate(grads_own, axis=0))]
    add x11 -> x17, other arithmetic: 4.03 us -> 20.2 us  [the longest x2 4.91 us: ffn_sum(): return keep + swap_core(send)]
  transfers between devices with their start and end apart: 52 -> 63, of which waited for: 23 -> 21; matrix products, arithmetic and copies ran while one was open for 29% -> 30% of each run, Pallas kernels for 0% -> 31%
where the time goes in v2:
time: 525 us; the launch traced here: 517 us
  Pallas kernels  168 us (32%)
  waiting for transfers between devices  110 us (21%)
  other arithmetic  104 us (20%)
  starting transfers between devices  59.2 us (11%)
  local copies, waits for them, and re-layouts  39.9 us (8%)
  matrix products  33.5 us (6%)
    ppermute x59, waiting for transfers between devices, swap(): lax.ppermute(block, axis, [(i, i ^ bit) for i in range(lax.axis_size(axis...  110 us
    pallas_call x3, Pallas kernels, feed_forward(): pl.pallas_call(functools.partial(ffn_kernel, len(pieces)), grid_spec=pltp...  64.1 us
    pallas_call x5, Pallas kernels, sum_halves(): pl.pallas_call(functools.partial(sum_kernel, width, parts), grid_spec=plt...  52.5 us
    ppermute x59, starting transfers between devices, swap(): lax.ppermute(block, axis, [(i, i ^ bit) for i in range(lax.axis_size(axis...  51.2 us
    pallas_call x10, Pallas kernels, halve_sum(): pl.pallas_call(step_kernel, grid_spec=pltpu.PrefetchScalarGridSpec(num_sc...  36 us
    unnamed x246, local copies, waits for them, and re-layouts  28.4 us
    dot_general x10, matrix products, dot(): return jnp.dot(left, right, preferred_element_type=jnp.float32)  18.9 us
    pallas_call x2, Pallas kernels, place_rows(): pl.pallas_call(functools.partial(place_kernel, pieces), grid_spec=pltpu.P...  15.6 us
  transfers between devices with their start and end apart: 63, of which 21 were waited for; matrix products, arithmetic and copies ran while one was open for 30% of the time, Pallas kernels for 31%

profile of v2, /device:TPU:0, one launch (start us, length us, event | category | flops | bytes accessed | tf_op | source)
XLA Modules:
  0.0 517.1 jit_solution(17797171269707671684)
XLA Ops:
  12.5 4.2 collective-permute-start
  18.3 3.6 fusion.128
  26.1 6.0 %multiply_convert_fusion.5 = (bf16[2048,256]{1,0:T(8,128)(2,1)S(1)}, f32[2048,256]{1,0:T(8,128)}, f32[2048,256]{1,0:T(8,128)}) fusion(f32[2048,256]{1,0:T(8,128)S(1)} %get-tuple-element.773, f32[2,256]{1,0:T(2,128)S(1)} %slice_multiply_fusion.2, f32[256]{0:T(256)S(1)} %bitcast.112, f32[256]{0:T(256)S(1)} %bitcast.110, f32[256]{0:T(256)S(1)} %bitcast.108, ...), kind=kOutput, calls=%fused_computation.46 | convolution fusion | flops 1078460416 | bytes 12063744 | tf_op jit(solution)/shard_map/dot_general | solution.py:55
  39.1 17.9 %collective-permute-done.1 = f32[1024,256]{1,0:T(8,128)S(1)} collective-permute-done((f32[1024,256]{1,0:T(8,128)S(1)}, f32[1024,256]{1,0:T(8,128)S(1)}, u32[]{:S(2)}, u32[]{:S(2)}) %collective-permute-start.1) | collective-permute-done | bytes 1048608 | tf_op jit(solution)/shard_map/ppermute | solution.py:20
  69.9 28.9 %shard_map.640 = (bf16[2048,1024]{1,0:T(8,128)(2,1)}, bf16[2048,1152]{1,0:T(8,128)(2,1)}, bf16[2048,1152]{1,0:T(8,128)(2,1)}, bf16[2048,1152]{1,0:T(8,128)(2,1)}...) custom-call(s32[4]{0:T(128)} %pad_add_fusion.2.place, ...), custom_call_target="tpu_custom_call" | custom-call | flops 30000001024 | bytes 10000000 | tf_op jit(solution)/shard_map/pallas_call | solution.py:178
  102.8 17.6 %shard_map.641 = (bf16[2048,1024]{1,0:T(8,128)(2,1)}, bf16[2048,1152]{1,0:T(8,128)(2,1)}, bf16[2048,1152]{1,0:T(8,128)(2,1)}, bf16[2048,1152]{1,0:T(8,128)(2,1)}...) custom-call(s32[2]{0:T(128)} %pad_add_fusion.3.place, ...), custom_call_target="tpu_custom_call", output_to_operand_aliasing={{0}: (7, {}), {1}: (8, {}), {2}: (9, {}), {3}: (10, {})} | custom-call | flops 30000001024 | bytes 10000000 | tf_op jit(solution)/shard_map/pallas_call | solution.py:178
  134.1 17.6 %shard_map.642 = (bf16[2048,1024]{1,0:T(8,128)(2,1)}, bf16[2048,1152]{1,0:T(8,128)(2,1)}, bf16[2048,1152]{1,0:T(8,128)(2,1)}, bf16[2048,1152]{1,0:T(8,128)(2,1)}...) custom-call(s32[2]{0:T(128)} %pad_add_fusion.4.place, ...), custom_call_target="tpu_custom_call", output_to_operand_aliasing={{0}: (7, {}), {1}: (8, {}), {2}: (9, {}), {3}: (10, {})} | custom-call | flops 30000001024 | bytes 10000000 | tf_op jit(solution)/shard_map/pallas_call | solution.py:178
  177.7 12.3 %shard_map.643 = (f32[512,1152]{1,0:T(8,128)}, f32[512,1152]{1,0:T(8,128)}) custom-call(s32[8]{0:T(128)} %pad_add_fusion.5.picks, bf16[2048,1024]{1,0:T(8,128)(2,1)} %refs_3_.4, bf16[2048,1024]{1,0:T(8,128)(2,1)} %refs_3_.4, bf16[2048,1024]{1,0:T(8,128)(2,1)} %refs_3_.4, bf16[2048,1024]{1,0:T(8,128)(2,1)} %refs_3_.4, ...), custom_call_target="tpu_custom_call" | custom-call | flops 999999995904 | bytes 10000000 | tf_op jit(solution)/shard_map/pallas_call | solution.py:270
  201.2 12.9 %shard_map.644 = (f32[512,1152]{1,0:T(8,128)}, f32[512,1152]{1,0:T(8,128)}) custom-call(s32[8]{0:T(128)} %pad_add_fusion.6.picks, bf16[2048,1024]{1,0:T(8,128)(2,1)} %get-tuple-element.418.refs_0_.refs_1_.refs_2_.refs_3_, bf16[2048,1024]{1,0:T(8,128)(2,1)} %get-tuple-element.418.refs_0_.refs_1_.refs_2_.refs_3_, ...), custom_call_target="tpu_custom_call" | custom-call | flops 999999995904 | bytes 10000000 | tf_op jit(solution)/shard_map/pallas_call | solution.py:270
  214.1 4.3 collective-permute-start.29
  228.3 12.3 %shard_map.645 = (f32[512,1152]{1,0:T(8,128)}, f32[512,1152]{1,0:T(8,128)}) custom-call(s32[8]{0:T(128)} %pad_add_fusion.6.picks, bf16[2048,1024]{1,0:T(8,128)(2,1)} %get-tuple-element.418.refs_0_.refs_1_.refs_2_.refs_3_, bf16[2048,1024]{1,0:T(8,128)(2,1)} %get-tuple-element.418.refs_0_.refs_1_.refs_2_.refs_3_, ...), custom_call_target="tpu_custom_call" | custom-call | flops 999999995904 | bytes 10000000 | tf_op jit(solution)/shard_map/pallas_call | solution.py:270
  254.5 5.9 %shard_map.646 = (f32[512,512]{1,0:T(8,128)}, f32[512,512]{1,0:T(8,128)}) custom-call(s32[8]{0:T(128)} %pad_add_fusion.6.picks, bf16[1024,1024]{1,0:T(8,128)(2,1)} %pad_maximum_fusion.3.refs_0_.refs_1_.refs_2_.refs_3_, bf16[1024,1024]{1,0:T(8,128)(2,1)} %pad_maximum_fusion.3.refs_0_.refs_1_.refs_2_.refs_3_, ...), custom_call_target="tpu_custom_call" | custom-call | flops 999999995904 | bytes 10000000 | tf_op jit(solution)/shard_map/pallas_call | solution.py:270
  273.8 4.3 shard_map.647
  282.1 9.1 %shard_map.648 = (f32[512,768]{1,0:T(8,128)}, f32[512,768]{1,0:T(8,128)}) custom-call(s32[8]{0:T(128)} %pad_add_fusion.6.picks, bf16[2048,1024]{1,0:T(8,128)(2,1)} %copy-done.11, bf16[2048,1024]{1,0:T(8,128)(2,1)} %copy-done.11, bf16[2048,1024]{1,0:T(8,128)(2,1)} %copy-done.11, bf16[2048,1024]{1,0:T(8,128)(2,1)} %copy-done.11, bf16[2048,768]{1,0:T(8,128)(2,1)} %copy-done.17), custom_call_target="tpu_custom_call" | custom-call | flops 999999995904 | bytes 10000000 | tf_op jit(solution)/shard_map/pallas_call | solution.py:270
  291.2 4.2 shard_map.650
  307.7 3.6 shard_map.649
  315.1 18.1 %collective-permute-done.36 = f32[256,1024]{1,0:T(8,128)} collective-permute-done((f32[256,1024]{1,0:T(8,128)}, f32[256,1024]{1,0:T(8,128)}, u32[]{:S(2)}, u32[]{:S(2)}) %collective-permute-start.36) | collective-permute-done | bytes 1048608 | tf_op jit(solution)/shard_map/ppermute | solution.py:20
  333.3 3.5 fusion.25
  342.2 4.4 shard_map.651
  346.6 9.1 %collective-permute-done.39 = f32[256,1024]{1,0:T(8,128)} collective-permute-done((f32[256,1024]{1,0:T(8,128)}, f32[256,1024]{1,0:T(8,128)}, u32[]{:S(2)}, u32[]{:S(2)}) %collective-permute-start.39) | collective-permute-done | bytes 1048608 | tf_op jit(solution)/shard_map/ppermute | solution.py:20
  367.2 4.3 fusion.28.refs_0_
  374.7 6.8 %collective-permute-done.41.refs_1_.refs_3_ = f32[2,128,1152]{2,1,0:T(8,128)} collective-permute-done((f32[2,128,1152]{2,1,0:T(8,128)}, f32[2,128,1152]{2,1,0:T(8,128)}, u32[]{:S(2)}, u32[]{:S(2)}) %collective-permute-start.41) | collective-permute-done | bytes 1179680 | tf_op jit(solution)/shard_map/ppermute | solution.py:20
  387.4 3.6 shard_map.653
  397.5 13.2 %collective-permute-done.47 = f32[1,128,1152]{2,1,0:T(8,128)} collective-permute-done((f32[1,128,1152]{2,1,0:T(8,128)}, f32[1,128,1152]{2,1,0:T(8,128)}, u32[]{:S(2)}, u32[]{:S(2)}) %collective-permute-start.47) | collective-permute-done | bytes 589856 | tf_op jit(solution)/shard_map/ppermute | solution.py:20
  414.6 4.0 collective-permute-done.45.refs_1_.refs_3_
  436.4 3.6 collective-permute-done.53
  444.2 4.9 collective-permute-done.49.refs_1_.refs_3_
  458.1 6.7 %collective-permute-done.60 = f32[16,128]{1,0:T(8,128)S(1)} collective-permute-done((f32[16,128]{1,0:T(8,128)S(1)}, f32[16,128]{1,0:T(8,128)S(1)}, u32[]{:S(2)}, u32[]{:S(2)}) %collective-permute-start.60) | collective-permute-done | bytes 8224 | tf_op jit(solution)/shard_map/ppermute | solution.py:20
  468.7 6.5 %collective-permute-done.55.refs_1_.refs_3_ = f32[2,128,512]{2,1,0:T(8,128)S(1)} collective-permute-done((f32[2,128,512]{2,1,0:T(8,128)}, f32[2,128,512]{2,1,0:T(8,128)S(1)}, u32[]{:S(2)}, u32[]{:S(2)}) %collective-permute-start.55) | collective-permute-done | bytes 524320 | tf_op jit(solution)/shard_map/ppermute | solution.py:20
  491.6 8.6 %shard_map.659 = f32[2048,1024]{1,0:T(8,128)} custom-call(s32[8]{0:T(128)S(1)} %stack.73.spots, f32[256,1024]{1,0:T(8,128)} %fusion.24.refs_0_, f32[256,1024]{1,0:T(8,128)} %fusion.19.refs_1_, f32[512,1024]{1,0:T(8,128)} %collective-permute-done.40.refs_2_, f32[256,1024]{1,0:T(8,128)} %collective-permute-done.38.refs_3_, ...), custom_call_target="tpu_custom_call" | custom-call | bytes 16777216 | tf_op jit(solution)/shard_map/pallas_call | solution.py:216
  503.2 3.5 collective-permute-done.62
  509.9 7.0 %shard_map.658 = bf16[2048,1024]{1,0:T(8,128)(2,1)} custom-call(s32[8]{0:T(128)S(1)} %stack.73.spots, f32[512,1024]{1,0:T(8,128)} %fusion.28.refs_0_, f32[512,1024]{1,0:T(8,128)} %collective-permute-done.54.refs_1_, f32[256,1024]{1,0:T(8,128)} %collective-permute-done.50.refs_2_, f32[256,1024]{1,0:T(8,128)} %collective-permute-done.57.refs_3_, ...), custom_call_target="tpu_custom_call" | custom-call | bytes 16777216 | tf_op jit(solution)/shard_map/pallas_call | solution.py:216
  (479 shorter events, 241.4 us)
Async XLA Ops:
  4.1 30.4 %collective-permute-start.2 = (f32[1024,768]{1,0:T(8,128)}, f32[1024,768]{1,0:T(8,128)}, u32[]{:S(2)}, u32[]{:S(2)}) collective-permute-start(f32[1024,768]{1,0:T(8,128)} %maximum_convert_fusion), channel_id=1, source_target_pairs={{0,1},{1,0},{2,3},{3,2},{4,5},{5,4},{6,7},{7,6},{8,9},{9,8},{10,11... | collective-permute-start | bytes 9437192 | tf_op jit(solution)/shard_map/ppermute | solution.py:20
  5.7 26.7 %collective-permute-start.3 = (f32[256,1024]{1,0:T(8,128)}, f32[256,1024]{1,0:T(8,128)}, u32[]{:S(2)}, u32[]{:S(2)}) collective-permute-start(f32[256,1024]{1,0:T(8,128)} %convert_element_type.155), channel_id=1, source_target_pairs={{0,2},{1,3},{2,0},{3,1},{4,6},{5,7},{6,4},{7,5},{8,10},{9,11},{10,... | collective-permute-start | bytes 3145736 | tf_op jit(solution)/shard_map/ppermute | solution.py:20
  10.5 28.6 %collective-permute-start.4 = (f32[8,256]{1,0:T(8,128)S(1)}, f32[8,256]{1,0:T(8,128)S(1)}, u32[]{:S(2)}, u32[]{:S(2)}) collective-permute-start(f32[8,256]{1,0:T(8,128)S(1)} %fusion.78), channel_id=1, source_target_pairs={{4,0},{8,4},{12,8},{16,12},{20,16},{24,20},{28,24},{5,1},{9,5},{13... | collective-permute-start | bytes 24584 | tf_op jit(solution)/shard_map/ppermute | solution.py:16
  32.1 24.8 %collective-permute-start.1 = (f32[1024,256]{1,0:T(8,128)S(1)}, f32[1024,256]{1,0:T(8,128)S(1)}, u32[]{:S(2)}, u32[]{:S(2)}) collective-permute-start(f32[1024,256]{1,0:T(8,128)S(1)} %dynamic-slice_convert_fusion), channel_id=1, source_target_pairs={{0,2},{1,3},{2,0},{3,1},{4,6},{5,7},{6,4},{7,5},{8,10},{9,11},{10,... | collective-permute-start | bytes 3145736 | tf_op jit(solution)/shard_map/ppermute | solution.py:20
  66.8 32.0 %collective-permute-start.10 = (f32[256,1024]{1,0:T(8,128)S(1)}, f32[256,1024]{1,0:T(8,128)}, u32[]{:S(2)}, u32[]{:S(2)}) collective-permute-start(f32[256,1024]{1,0:T(8,128)S(1)} %get-tuple-element.768.refs_0_), channel_id=1, source_target_pairs={{0,2},{1,3},{2,0},{3,1},{4,6},{5,7},{6,4},{7,5},{8,10},{9,11},{10,... | collective-permute-start | bytes 3145736 | tf_op jit(solution)/shard_map/ppermute | solution.py:20
  99.6 30.5 %collective-permute-start.15 = (f32[256,1024]{1,0:T(8,128)}, f32[256,1024]{1,0:T(8,128)}, u32[]{:S(2)}, u32[]{:S(2)}) collective-permute-start(f32[256,1024]{1,0:T(8,128)} %copy-done.53), channel_id=1, source_target_pairs={{0,2},{1,3},{2,0},{3,1},{4,6},{5,7},{6,4},{7,5},{8,10},{9,11},{10,... | collective-permute-start | bytes 3145736 | tf_op jit(solution)/shard_map/ppermute | solution.py:20
  99.9 27.6 %collective-permute-start.9 = (f32[512,1024]{1,0:T(8,128)}, f32[512,1024]{1,0:T(8,128)}, u32[]{:S(2)}, u32[]{:S(2)}) collective-permute-start(f32[512,1024]{1,0:T(8,128)} %get-tuple-element.334), channel_id=1, source_target_pairs={{0,1},{1,0},{2,3},{3,2},{4,5},{5,4},{6,7},{7,6},{8,9},{9,8},{10,11... | collective-permute-start | bytes 6291464 | tf_op jit(solution)/shard_map/ppermute | solution.py:20
  133.8 38.5 %collective-permute-start.14 = (f32[256,1024]{1,0:T(8,128)}, f32[256,1024]{1,0:T(8,128)}, u32[]{:S(2)}, u32[]{:S(2)}) collective-permute-start(f32[256,1024]{1,0:T(8,128)} %maximum_add_fusion.2), channel_id=1, source_target_pairs={{0,2},{1,3},{2,0},{3,1},{4,6},{5,7},{6,4},{7,5},{8,10},{9,11},{10,... | collective-permute-start | bytes 3145736 | tf_op jit(solution)/shard_map/ppermute | solution.py:20
  189.9 31.2 %collective-permute-start.20 = (f32[256,1024]{1,0:T(8,128)}, f32[256,1024]{1,0:T(8,128)}, u32[]{:S(2)}, u32[]{:S(2)}) collective-permute-start(f32[256,1024]{1,0:T(8,128)} %maximum_add_fusion.3), channel_id=1, source_target_pairs={{0,2},{1,3},{2,0},{3,1},{4,6},{5,7},{6,4},{7,5},{8,10},{9,11},{10,... | collective-permute-start | bytes 3145736 | tf_op jit(solution)/shard_map/ppermute | solution.py:20
  196.4 31.4 %collective-permute-start.24 = (f32[512,256]{1,0:T(8,128)}, f32[512,256]{1,0:T(8,128)}, u32[]{:S(2)}, u32[]{:S(2)}) collective-permute-start(f32[512,256]{1,0:T(8,128)} %fusion.130), channel_id=1, source_target_pairs={{0,2},{1,3},{2,0},{3,1},{4,6},{5,7},{6,4},{7,5},{8,10},{9,11},{10,... | collective-permute-start | bytes 1572872 | tf_op jit(solution)/shard_map/ppermute | solution.py:20
  214.1 59.6 %collective-permute-start.29 = (f32[4,128,1152]{2,1,0:T(8,128)}, f32[4,128,1152]{2,1,0:T(8,128)}, u32[]{:S(2)}, u32[]{:S(2)}) collective-permute-start(f32[4,128,1152]{2,1,0:T(8,128)} %bitcast.114), channel_id=1, source_target_pairs={{0,4},{4,0},{8,12},{12,8},{16,20},{20,16},{24,28},{28,24},{1,5},{5... | collective-permute-start | bytes 7077896 | tf_op jit(solution)/shard_map/ppermute | solution.py:20
  218.5 55.3 %collective-permute-start.30 = (f32[4,128,1152]{2,1,0:T(8,128)}, f32[4,128,1152]{2,1,0:T(8,128)}, u32[]{:S(2)}, u32[]{:S(2)}) collective-permute-start(f32[4,128,1152]{2,1,0:T(8,128)} %bitcast.15), channel_id=1, source_target_pairs={{0,8},{4,12},{8,0},{12,4},{16,24},{20,28},{24,16},{28,20},{1,9},{5... | collective-permute-start | bytes 7077896 | tf_op jit(solution)/shard_map/ppermute | solution.py:20
  253.6 61.6 %collective-permute-start.34 = (f32[256,1024]{1,0:T(8,128)}, f32[256,1024]{1,0:T(8,128)}, u32[]{:S(2)}, u32[]{:S(2)}) collective-permute-start(f32[256,1024]{1,0:T(8,128)} %add.595), channel_id=1, source_target_pairs={{0,2},{1,3},{2,0},{3,1},{4,6},{5,7},{6,4},{7,5},{8,10},{9,11},{10,... | collective-permute-start | bytes 3145736 | tf_op jit(solution)/shard_map/ppermute | solution.py:20
  260.4 45.2 %collective-permute-start.33 = (f32[256,1024]{1,0:T(8,128)}, f32[256,1024]{1,0:T(8,128)}, u32[]{:S(2)}, u32[]{:S(2)}) collective-permute-start(f32[256,1024]{1,0:T(8,128)} %add.596), channel_id=1, source_target_pairs={{0,2},{1,3},{2,0},{3,1},{4,6},{5,7},{6,4},{7,5},{8,10},{9,11},{10,... | collective-permute-start | bytes 3145736 | tf_op jit(solution)/shard_map/ppermute | solution.py:20
  278.1 28.8 %collective-permute-start.32 = (f32[2,128,1152]{2,1,0:T(8,128)}, f32[2,128,1152]{2,1,0:T(8,128)}, u32[]{:S(2)}, u32[]{:S(2)}) collective-permute-start(f32[2,128,1152]{2,1,0:T(8,128)} %get-tuple-element.468), channel_id=1, source_target_pairs={{0,8},{4,12},{8,0},{12,4},{16,24},{20,28},{24,16},{28,20},{1,9},{5... | collective-permute-start | bytes 3538952 | tf_op jit(solution)/shard_map/ppermute | solution.py:20
  279.8 59.4 %collective-permute-start.35 = (f32[4,128,1152]{2,1,0:T(8,128)}, f32[4,128,1152]{2,1,0:T(8,128)}, u32[]{:S(2)}, u32[]{:S(2)}) collective-permute-start(f32[4,128,1152]{2,1,0:T(8,128)} %bitcast.19), channel_id=1, source_target_pairs={{0,4},{4,0},{8,12},{12,8},{16,20},{20,16},{24,28},{28,24},{1,5},{5... | collective-permute-start | bytes 7077896 | tf_op jit(solution)/shard_map/ppermute | solution.py:20
  306.9 26.4 %collective-permute-start.36 = (f32[256,1024]{1,0:T(8,128)}, f32[256,1024]{1,0:T(8,128)}, u32[]{:S(2)}, u32[]{:S(2)}) collective-permute-start(f32[256,1024]{1,0:T(8,128)} %fusion.38), channel_id=1, source_target_pairs={{0,2},{1,3},{2,0},{3,1},{4,6},{5,7},{6,4},{7,5},{8,10},{9,11},{10,... | collective-permute-start | bytes 3145736 | tf_op jit(solution)/shard_map/ppermute | solution.py:20
  311.4 44.3 %collective-permute-start.39 = (f32[256,1024]{1,0:T(8,128)}, f32[256,1024]{1,0:T(8,128)}, u32[]{:S(2)}, u32[]{:S(2)}) collective-permute-start(f32[256,1024]{1,0:T(8,128)} %fusion.34), channel_id=1, source_target_pairs={{0,2},{1,3},{2,0},{3,1},{4,6},{5,7},{6,4},{7,5},{8,10},{9,11},{10,... | collective-permute-start | bytes 3145736 | tf_op jit(solution)/shard_map/ppermute | solution.py:20
  312.5 53.3 %collective-permute-start.42 = (f32[1,128,1152]{2,1,0:T(8,128)}, f32[1,128,1152]{2,1,0:T(8,128)}, u32[]{:S(2)}, u32[]{:S(2)}) collective-permute-start(f32[1,128,1152]{2,1,0:T(8,128)} %get-tuple-element.510), channel_id=1, source_target_pairs={{0,16},{4,20},{8,24},{12,28},{16,0},{20,4},{24,8},{28,12},{1,17},{... | collective-permute-start | bytes 1769480 | tf_op jit(solution)/shard_map/ppermute | solution.py:20
  339.1 48.3 %collective-permute-start.37 = (f32[4,128,768]{2,1,0:T(8,128)}, f32[4,128,768]{2,1,0:T(8,128)}, u32[]{:S(2)}, u32[]{:S(2)}) collective-permute-start(f32[4,128,768]{2,1,0:T(8,128)} %bitcast.26), channel_id=1, source_target_pairs={{0,4},{4,0},{8,12},{12,8},{16,20},{20,16},{24,28},{28,24},{1,5},{5... | collective-permute-start | bytes 4718600 | tf_op jit(solution)/shard_map/ppermute | solution.py:20
  341.5 45.9 %collective-permute-start.38 = (f32[256,1024]{1,0:T(8,128)}, f32[256,1024]{1,0:T(8,128)}, u32[]{:S(2)}, u32[]{:S(2)}) collective-permute-start(f32[256,1024]{1,0:T(8,128)} %fusion.24.refs_0_), channel_id=1, source_target_pairs={{0,2},{1,3},{2,0},{3,1},{4,6},{5,7},{6,4},{7,5},{8,10},{9,11},{10,... | collective-permute-start | bytes 3145736 | tf_op jit(solution)/shard_map/ppermute | solution.py:20
  355.7 25.8 %collective-permute-start.41 = (f32[2,128,1152]{2,1,0:T(8,128)}, f32[2,128,1152]{2,1,0:T(8,128)}, u32[]{:S(2)}, u32[]{:S(2)}) collective-permute-start(f32[2,128,1152]{2,1,0:T(8,128)} %get-tuple-element.509), channel_id=1, source_target_pairs={{0,8},{4,12},{8,0},{12,4},{16,24},{20,28},{24,16},{28,20},{1,9},{5... | collective-permute-start | bytes 3538952 | tf_op jit(solution)/shard_map/ppermute | solution.py:20
  365.9 44.8 %collective-permute-start.46 = (f32[256,1024]{1,0:T(8,128)}, f32[256,1024]{1,0:T(8,128)}, u32[]{:S(2)}, u32[]{:S(2)}) collective-permute-start(f32[256,1024]{1,0:T(8,128)} %fusion.19.refs_1_), channel_id=1, source_target_pairs={{0,2},{1,3},{2,0},{3,1},{4,6},{5,7},{6,4},{7,5},{8,10},{9,11},{10,... | collective-permute-start | bytes 3145736 | tf_op jit(solution)/shard_map/ppermute | solution.py:20
  384.8 25.8 %collective-permute-start.47 = (f32[1,128,1152]{2,1,0:T(8,128)}, f32[1,128,1152]{2,1,0:T(8,128)}, u32[]{:S(2)}, u32[]{:S(2)}) collective-permute-start(f32[1,128,1152]{2,1,0:T(8,128)} %get-tuple-element.532), channel_id=1, source_target_pairs={{0,16},{4,20},{8,24},{12,28},{16,0},{20,4},{24,8},{28,12},{1,17},{... | collective-permute-start | bytes 1769480 | tf_op jit(solution)/shard_map/ppermute | solution.py:20
  391.1 27.5 %collective-permute-start.45 = (f32[2,128,768]{2,1,0:T(8,128)}, f32[2,128,768]{2,1,0:T(8,128)S(1)}, u32[]{:S(2)}, u32[]{:S(2)}) collective-permute-start(f32[2,128,768]{2,1,0:T(8,128)} %get-tuple-element.530), channel_id=1, source_target_pairs={{0,8},{4,12},{8,0},{12,4},{16,24},{20,28},{24,16},{28,20},{1,9},{5... | collective-permute-start | bytes 2359304 | tf_op jit(solution)/shard_map/ppermute | solution.py:20
  395.4 31.3 %collective-permute-start.43 = (f32[2,128,1152]{2,1,0:T(8,128)}, f32[2,128,1152]{2,1,0:T(8,128)}, u32[]{:S(2)}, u32[]{:S(2)}) collective-permute-start(f32[2,128,1152]{2,1,0:T(8,128)} %get-tuple-element.522), channel_id=1, source_target_pairs={{0,4},{4,0},{8,12},{12,8},{16,20},{20,16},{24,28},{28,24},{1,5},{5... | collective-permute-start | bytes 3538952 | tf_op jit(solution)/shard_map/ppermute | solution.py:20
  397.0 25.5 %collective-permute-start.44 = (f32[22,128]{1,0:T(8,128)}, f32[22,128]{1,0:T(8,128)}, u32[]{:S(2)}, u32[]{:S(2)}) collective-permute-start(f32[22,128]{1,0:T(8,128)} %pad_maximum_fusion.8), channel_id=1, source_target_pairs={{0,4},{4,0},{8,12},{12,8},{16,20},{20,16},{24,28},{28,24},{1,5},{5... | collective-permute-start | bytes 33800 | tf_op jit(solution)/shard_map/ppermute | solution.py:20
  410.6 30.6 %collective-permute-start.50 = (f32[256,1024]{1,0:T(8,128)}, f32[256,1024]{1,0:T(8,128)}, u32[]{:S(2)}, u32[]{:S(2)}) collective-permute-start(f32[256,1024]{1,0:T(8,128)} %get-tuple-element.550), channel_id=1, source_target_pairs={{0,2},{1,3},{2,0},{3,1},{4,6},{5,7},{6,4},{7,5},{8,10},{9,11},{10,... | collective-permute-start | bytes 3145736 | tf_op jit(solution)/shard_map/ppermute | solution.py:20
  414.6 54.1 %collective-permute-start.56 = (f32[512,1024]{1,0:T(8,128)}, f32[512,1024]{1,0:T(8,128)}, u32[]{:S(2)}, u32[]{:S(2)}) collective-permute-start(f32[512,1024]{1,0:T(8,128)} %pad_maximum_fusion.5), channel_id=1, source_target_pairs={{0,1},{1,0},{2,3},{3,2},{4,5},{5,4},{6,7},{7,6},{8,9},{9,8},{10,11... | collective-permute-start | bytes 6291464 | tf_op jit(solution)/shard_map/ppermute | solution.py:20
  440.0 38.7 %collective-permute-start.57 = (f32[256,1024]{1,0:T(8,128)}, f32[256,1024]{1,0:T(8,128)}, u32[]{:S(2)}, u32[]{:S(2)}) collective-permute-start(f32[256,1024]{1,0:T(8,128)} %get-tuple-element.577), channel_id=1, source_target_pairs={{0,2},{1,3},{2,0},{3,1},{4,6},{5,7},{6,4},{7,5},{8,10},{9,11},{10,... | collective-permute-start | bytes 3145736 | tf_op jit(solution)/shard_map/ppermute | solution.py:20
  441.2 27.5 %collective-permute-start.48 = (f32[1,128,1152]{2,1,0:T(8,128)}, f32[1,128,1152]{2,1,0:T(8,128)}, u32[]{:S(2)}, u32[]{:S(2)}) collective-permute-start(f32[1,128,1152]{2,1,0:T(8,128)} %get-tuple-element.547), channel_id=1, source_target_pairs={{0,16},{4,20},{8,24},{12,28},{16,0},{20,4},{24,8},{28,12},{1,17},{... | collective-permute-start | bytes 1769480 | tf_op jit(solution)/shard_map/ppermute | solution.py:20
  482.0 27.9 %collective-permute-start.58 = (f32[512,1024]{1,0:T(8,128)}, f32[512,1024]{1,0:T(8,128)S(1)}, u32[]{:S(2)}, u32[]{:S(2)}) collective-permute-start(f32[512,1024]{1,0:T(8,128)} %pad_maximum_fusion.6), channel_id=1, source_target_pairs={{0,1},{1,0},{2,3},{3,2},{4,5},{5,4},{6,7},{7,6},{8,9},{9,8},{10,11... | collective-permute-start | bytes 6291464 | tf_op jit(solution)/shard_map/ppermute | solution.py:20
  (148 other events, 1314.4 us)

commit v3 on v2

--- a/solution.py
+++ b/solution.py
@@ -74,6 +74,25 @@
     square_hat = square_new / (1.0 - 0.95**3)
     weight_new = weight - rate * (mean_hat / (jnp.sqrt(square_hat) + 1e-08) + decay * weight)
     return (weight_new, mean_new, square_new)
+
+
+def turned_kernel(decay, rate, turned, weight, mean, square, *outs):
+    grad = turned[...].T
+    updated = adamw(weight[...].astype(jnp.float32), grad, mean[...], square[...], decay, rate)
+    for out, value in zip(outs, (grad,) + updated):
+        out[...] = value
+
+
+def adamw_turned(turned, weight, mean, square, decay, rate):
+    if mean.shape[1] % 128 != 0:
+        grad = turned.T
+        return (grad,) + adamw(weight.astype(jnp.float32), grad, mean, square, decay, rate)
+    return pl.pallas_call(
+        functools.partial(turned_kernel, decay, rate),
+        out_shape=[jax.ShapeDtypeStruct(mean.shape, jnp.float32)] * 4,
+        compiler_params=pltpu.CompilerParams(vmem_limit_bytes=24 * 2**20),
+        cost_estimate=pl.CostEstimate(flops=10**9, bytes_accessed=10**7, transcendentals=0),
+    )(turned, weight, mean, square)
 
 
 def norm_back(dnormed, normed, inverse):
@@ -656,15 +675,12 @@
         count,
         jnp.float32,
     )
+    grad_tokens = clock.passes(grad_tokens)
     outw.finish(clock)
     outw.start(clock)
     block_near = clock.passes(block_near)
     block_across[1] = clock.passes(block_across[1])
-    block_corner = swap_core(jnp.concatenate(block_across, axis=0))
-    grad_outw_both = outw.final(clock)
-    grad_outw = grad_outw_both[:, :quarter] + swap_y(grad_outw_both[:, quarter:])
-    grad_outw = lax.optimization_barrier(grad_outw.T)
-    grad_down = lax.optimization_barrier(grad_down.T)
+    block_corner = clock.passes(swap_core(jnp.concatenate(block_across, axis=0)))
     block_out = place_rows(
         [block_own, block_near, *block_across, block_corner],
         [piece(k, j, w) for k in (upper, 1 - upper) for w in (core, 1 - core) for j in range(2)],
@@ -672,14 +688,14 @@
         count,
         jnp.bfloat16,
     )
+    block_out = clock.passes(block_out)
+    grad_outw_both = outw.final(clock)
+    grad_outw = grad_outw_both[:, :quarter] + swap_y(grad_outw_both[:, quarter:])
 
     width = features // lax.axis_size("seq")
 
     def rows_of(weight):
         return lax.dynamic_slice_in_dim(weight, place * width, width, 0).astype(jnp.float32)
-
-    def columns_of(weight):
-        return lax.dynamic_slice_in_dim(weight, place * width, width, 1).astype(jnp.float32)
 
     params = [
         clock.value,
@@ -687,11 +703,11 @@
         rows_of(w_cgate),
         rows_of(w_input),
         kernel,
-        columns_of(w_output),
+        None,
         gain_ffn,
         rows_of(w_gate),
         rows_of(w_up),
-        columns_of(w_down),
+        None,
     ]
     grads = [
         gains[0],
@@ -721,15 +737,17 @@
     rates = [0.2, 0.01, 0.01, 0.01, 0.2, 0.01, 0.2, 0.01, 0.01, 0.01]
     outs = [block_out, grad_tokens]
     for index in range(10):
-        weight_new, mean_new, square_new = adamw(
-            params[index],
-            grads[index],
-            moments[index][0],
-            moments[index][1],
-            decays[index],
-            rates[index],
-        )
-        outs = outs + [grads[index], weight_new, mean_new, square_new]
+        mean, square = moments[index]
+        if index in (5, 9):
+            weight = lax.dynamic_slice_in_dim(
+                w_output if index == 5 else w_down, place * width, width, 1
+            )
+            outs += list(
+                adamw_turned(grads[index], weight, mean, square, decays[index], rates[index])
+            )
+            continue
+        updated = adamw(params[index], grads[index], mean, square, decays[index], rates[index])
+        outs += [grads[index], *updated]
     return tuple(outs)
 
 

time: 525 us -> 506 us (0.964)
  local copies, waits for them, and re-layouts: 39.9 us -> 17.9 us
  other arithmetic: 104 us -> 97.4 us
    unnamed x246 -> x248, local copies, waits for them, and re-layouts: 28.4 us -> 9.09 us
    sub x7 -> x5, other arithmetic: 10.6 us -> 8.75 us  [adamw(): weight - rate * (mean_hat / (jnp.sqrt(square_hat) + 1e-08) + decay * weight)]
  transfers between devices with their start and end apart: 63 -> 63, of which waited for: 21 -> 22; matrix products, arithmetic and copies ran while one was open for 30% -> 25% of each run, Pallas kernels for 31% -> 34%
where the time goes in v3:
time: 506 us; the launch traced here: 498 us
  Pallas kernels  170 us (34%)
  waiting for transfers between devices  113 us (22%)
  other arithmetic  97.4 us (19%)
  starting transfers between devices  61.1 us (12%)
  matrix products  35.1 us (7%)
  local copies, waits for them, and re-layouts  17.9 us (4%)
    ppermute x59, waiting for transfers between devices, swap(): lax.ppermute(block, axis, [(i, i ^ bit) for i in range(lax.axis_size(axis...  113 us
    pallas_call x3, Pallas kernels, feed_forward(): pl.pallas_call(functools.partial(ffn_kernel, len(pieces)), grid_spec=pltp...  63.7 us
    ppermute x59, starting transfers between devices, swap(): lax.ppermute(block, axis, [(i, i ^ bit) for i in range(lax.axis_size(axis...  53.1 us
    pallas_call x5, Pallas kernels, sum_halves(): pl.pallas_call(functools.partial(sum_kernel, width, parts), grid_spec=plt...  52.4 us
    pallas_call x10, Pallas kernels, halve_sum(): pl.pallas_call(step_kernel, grid_spec=pltpu.PrefetchScalarGridSpec(num_sc...  35.7 us
    dot_general x10, matrix products, dot(): return jnp.dot(left, right, preferred_element_type=jnp.float32)  19.8 us
    pallas_call x2, Pallas kernels, place_rows(): pl.pallas_call(functools.partial(place_kernel, pieces), grid_spec=pltpu.P...  15.9 us
    convert_element_type x7, other arithmetic, wide(): return block.astype(jnp.float32)  15.5 us
  transfers between devices with their start and end apart: 63, of which 22 were waited for; matrix products, arithmetic and copies ran while one was open for 25% of the time, Pallas kernels for 34%

profile of v3, /device:TPU:0, one launch (start us, length us, event | category | flops | bytes accessed | tf_op | source)
XLA Modules:
  0.0 498.5 jit_solution(4836067652241538123)
XLA Ops:
  0.7 3.4 maximum_convert_fusion
  12.5 4.2 collective-permute-start
  18.3 3.6 fusion.119
  26.1 5.9 %multiply_convert_fusion.5 = (bf16[2048,256]{1,0:T(8,128)(2,1)S(1)}, f32[2048,256]{1,0:T(8,128)}, f32[2048,256]{1,0:T(8,128)}) fusion(f32[2048,256]{1,0:T(8,128)S(1)} %get-tuple-element.711, f32[2,256]{1,0:T(2,128)S(1)} %slice_multiply_fusion.2, f32[256]{0:T(256)S(1)} %bitcast.108, f32[256]{0:T(256)S(1)} %bitcast.106, f32[256]{0:T(256)S(1)} %bitcast.104, ...), kind=kOutput, calls=%fused_computation.46 | convolution fusion | flops 1078460416 | bytes 12063744 | tf_op jit(solution)/shard_map/dot_general | solution.py:55
  39.1 17.8 %collective-permute-done.1 = f32[1024,256]{1,0:T(8,128)S(1)} collective-permute-done((f32[1024,256]{1,0:T(8,128)S(1)}, f32[1024,256]{1,0:T(8,128)S(1)}, u32[]{:S(2)}, u32[]{:S(2)}) %collective-permute-start.1) | collective-permute-done | bytes 1048608 | tf_op jit(solution)/shard_map/ppermute | solution.py:20
  71.0 28.8 %shard_map.640 = (bf16[2048,1024]{1,0:T(8,128)(2,1)}, bf16[2048,1152]{1,0:T(8,128)(2,1)}, bf16[2048,1152]{1,0:T(8,128)(2,1)}, bf16[2048,1152]{1,0:T(8,128)(2,1)}...) custom-call(s32[4]{0:T(128)} %pad_add_fusion.2.place, ...), custom_call_target="tpu_custom_call" | custom-call | flops 30000001024 | bytes 10000000 | tf_op jit(solution)/shard_map/pallas_call | solution.py:197
  103.7 17.5 %shard_map.641 = (bf16[2048,1024]{1,0:T(8,128)(2,1)}, bf16[2048,1152]{1,0:T(8,128)(2,1)}, bf16[2048,1152]{1,0:T(8,128)(2,1)}, bf16[2048,1152]{1,0:T(8,128)(2,1)}...) custom-call(s32[2]{0:T(128)} %pad_add_fusion.3.place, ...), custom_call_target="tpu_custom_call", output_to_operand_aliasing={{0}: (7, {}), {1}: (8, {}), {2}: (9, {}), {3}: (10, {})} | custom-call | flops 30000001024 | bytes 10000000 | tf_op jit(solution)/shard_map/pallas_call | solution.py:197
  130.1 17.4 %shard_map.642 = (bf16[2048,1024]{1,0:T(8,128)(2,1)}, bf16[2048,1152]{1,0:T(8,128)(2,1)}, bf16[2048,1152]{1,0:T(8,128)(2,1)}, bf16[2048,1152]{1,0:T(8,128)(2,1)}...) custom-call(s32[2]{0:T(128)} %pad_add_fusion.4.place, ...), custom_call_target="tpu_custom_call", output_to_operand_aliasing={{0}: (7, {}), {1}: (8, {}), {2}: (9, {}), {3}: (10, {})} | custom-call | flops 30000001024 | bytes 10000000 | tf_op jit(solution)/shard_map/pallas_call | solution.py:197
  163.3 12.3 %shard_map.643 = (f32[512,1152]{1,0:T(8,128)}, f32[512,1152]{1,0:T(8,128)}) custom-call(s32[8]{0:T(128)} %pad_add_fusion.5.picks, bf16[2048,1024]{1,0:T(8,128)(2,1)} %refs_3_.4, bf16[2048,1024]{1,0:T(8,128)(2,1)} %refs_3_.4, bf16[2048,1024]{1,0:T(8,128)(2,1)} %refs_3_.4, bf16[2048,1024]{1,0:T(8,128)(2,1)} %refs_3_.4, ...), custom_call_target="tpu_custom_call" | custom-call | flops 999999995904 | bytes 10000000 | tf_op jit(solution)/shard_map/pallas_call | solution.py:289
  186.8 12.9 %shard_map.644 = (f32[512,1152]{1,0:T(8,128)}, f32[512,1152]{1,0:T(8,128)}) custom-call(s32[8]{0:T(128)} %pad_add_fusion.6.picks, bf16[2048,1024]{1,0:T(8,128)(2,1)} %get-tuple-element.432.refs_0_.refs_1_.refs_2_.refs_3_, bf16[2048,1024]{1,0:T(8,128)(2,1)} %get-tuple-element.432.refs_0_.refs_1_.refs_2_.refs_3_, ...), custom_call_target="tpu_custom_call" | custom-call | flops 999999995904 | bytes 10000000 | tf_op jit(solution)/shard_map/pallas_call | solution.py:289
  199.7 3.7 collective-permute-start.29
  213.1 12.3 %shard_map.645 = (f32[512,1152]{1,0:T(8,128)}, f32[512,1152]{1,0:T(8,128)}) custom-call(s32[8]{0:T(128)} %pad_add_fusion.6.picks, bf16[2048,1024]{1,0:T(8,128)(2,1)} %get-tuple-element.432.refs_0_.refs_1_.refs_2_.refs_3_, bf16[2048,1024]{1,0:T(8,128)(2,1)} %get-tuple-element.432.refs_0_.refs_1_.refs_2_.refs_3_, ...), custom_call_target="tpu_custom_call" | custom-call | flops 999999995904 | bytes 10000000 | tf_op jit(solution)/shard_map/pallas_call | solution.py:289
  239.2 5.9 %shard_map.646 = (f32[512,512]{1,0:T(8,128)}, f32[512,512]{1,0:T(8,128)}) custom-call(s32[8]{0:T(128)} %pad_add_fusion.6.picks, bf16[1024,1024]{1,0:T(8,128)(2,1)} %pad_maximum_fusion.3.refs_0_.refs_1_.refs_2_.refs_3_, bf16[1024,1024]{1,0:T(8,128)(2,1)} %pad_maximum_fusion.3.refs_0_.refs_1_.refs_2_.refs_3_, ...), custom_call_target="tpu_custom_call" | custom-call | flops 999999995904 | bytes 10000000 | tf_op jit(solution)/shard_map/pallas_call | solution.py:289
  258.4 4.3 shard_map.647
  266.8 9.1 %shard_map.648 = (f32[512,768]{1,0:T(8,128)}, f32[512,768]{1,0:T(8,128)}) custom-call(s32[8]{0:T(128)} %pad_add_fusion.6.picks, bf16[2048,1024]{1,0:T(8,128)(2,1)} %copy-done.17, bf16[2048,1024]{1,0:T(8,128)(2,1)} %copy-done.17, bf16[2048,1024]{1,0:T(8,128)(2,1)} %copy-done.17, bf16[2048,1024]{1,0:T(8,128)(2,1)} %copy-done.17, bf16[2048,768]{1,0:T(8,128)(2,1)} %copy-done.23), custom_call_target="tpu_custom_call" | custom-call | flops 999999995904 | bytes 10000000 | tf_op jit(solution)/shard_map/pallas_call | solution.py:289
  275.9 4.2 shard_map.650
  292.3 3.6 shard_map.649
  299.8 18.1 %collective-permute-done.36 = f32[256,1024]{1,0:T(8,128)} collective-permute-done((f32[256,1024]{1,0:T(8,128)}, f32[256,1024]{1,0:T(8,128)}, u32[]{:S(2)}, u32[]{:S(2)}) %collective-permute-start.36) | collective-permute-done | bytes 1048608 | tf_op jit(solution)/shard_map/ppermute | solution.py:20
  317.9 3.5 fusion.25
  326.9 4.4 shard_map.651
  331.4 9.0 %collective-permute-done.39 = f32[256,1024]{1,0:T(8,128)} collective-permute-done((f32[256,1024]{1,0:T(8,128)}, f32[256,1024]{1,0:T(8,128)}, u32[]{:S(2)}, u32[]{:S(2)}) %collective-permute-start.39) | collective-permute-done | bytes 1048608 | tf_op jit(solution)/shard_map/ppermute | solution.py:20
  341.9 3.5 fusion.20
  351.9 4.6 fusion.28.refs_0_
  359.6 6.5 %collective-permute-done.41.refs_1_.refs_3_ = f32[2,128,1152]{2,1,0:T(8,128)} collective-permute-done((f32[2,128,1152]{2,1,0:T(8,128)}, f32[2,128,1152]{2,1,0:T(8,128)}, u32[]{:S(2)}, u32[]{:S(2)}) %collective-permute-start.41) | collective-permute-done | bytes 1179680 | tf_op jit(solution)/shard_map/ppermute | solution.py:20
  369.5 3.6 shard_map.653
  380.9 20.3 %collective-permute-done.47 = f32[1,128,1152]{2,1,0:T(8,128)S(1)} collective-permute-done((f32[1,128,1152]{2,1,0:T(8,128)S(1)}, f32[1,128,1152]{2,1,0:T(8,128)S(1)}, u32[]{:S(2)}, u32[]{:S(2)}) %collective-permute-start.47) | collective-permute-done | bytes 589856 | tf_op jit(solution)/shard_map/ppermute | solution.py:20
  405.9 3.4 collective-permute-start.51
  424.8 9.8 %collective-permute-done.49.refs_1_.refs_3_ = f32[4,128,512]{2,1,0:T(8,128)} collective-permute-done((f32[4,128,512]{2,1,0:T(8,128)}, f32[4,128,512]{2,1,0:T(8,128)}, u32[]{:S(2)}, u32[]{:S(2)}) %collective-permute-start.49) | collective-permute-done | bytes 1048608 | tf_op jit(solution)/shard_map/ppermute | solution.py:20
  441.6 11.3 %collective-permute-done.48 = f32[1,128,1152]{2,1,0:T(8,128)} collective-permute-done((f32[1,128,1152]{2,1,0:T(8,128)}, f32[1,128,1152]{2,1,0:T(8,128)}, u32[]{:S(2)}, u32[]{:S(2)}) %collective-permute-start.48) | collective-permute-done | bytes 589856 | tf_op jit(solution)/shard_map/ppermute | solution.py:20
  453.0 8.8 %shard_map.657 = f32[2048,1024]{1,0:T(8,128)} custom-call(s32[8]{0:T(128)S(1)} %stack.73.spots, f32[256,1024]{1,0:T(8,128)} %fusion.24.refs_0_, f32[256,1024]{1,0:T(8,128)} %fusion.19.refs_1_, f32[512,1024]{1,0:T(8,128)} %collective-permute-done.40.refs_2_, f32[256,1024]{1,0:T(8,128)} %collective-permute-done.38.refs_3_, ...), custom_call_target="tpu_custom_call" | custom-call | bytes 16777216 | tf_op jit(solution)/shard_map/pallas_call | solution.py:235
  483.4 7.1 %shard_map.659 = bf16[2048,1024]{1,0:T(8,128)(2,1)} custom-call(s32[8]{0:T(128)S(1)} %copy-done.1, f32[512,1024]{1,0:T(8,128)} %fusion.28.refs_0_, f32[512,1024]{1,0:T(8,128)} %collective-permute-done.54.refs_1_, f32[256,1024]{1,0:T(8,128)} %collective-permute-done.50.refs_2_, f32[256,1024]{1,0:T(8,128)} %collective-permute-done.57.refs_3_, ...), custom_call_target="tpu_custom_call" | custom-call | bytes 16777216 | tf_op jit(solution)/shard_map/pallas_call | solution.py:235
  493.7 3.6 collective-permute-done.62
  (480 shorter events, 211.0 us)
Async XLA Ops:
  4.1 30.4 %collective-permute-start.2 = (f32[1024,768]{1,0:T(8,128)}, f32[1024,768]{1,0:T(8,128)}, u32[]{:S(2)}, u32[]{:S(2)}) collective-permute-start(f32[1024,768]{1,0:T(8,128)} %maximum_convert_fusion), channel_id=1, source_target_pairs={{0,1},{1,0},{2,3},{3,2},{4,5},{5,4},{6,7},{7,6},{8,9},{9,8},{10,11... | collective-permute-start | bytes 9437192 | tf_op jit(solution)/shard_map/ppermute | solution.py:20
  5.7 26.7 %collective-permute-start.3 = (f32[256,1024]{1,0:T(8,128)}, f32[256,1024]{1,0:T(8,128)}, u32[]{:S(2)}, u32[]{:S(2)}) collective-permute-start(f32[256,1024]{1,0:T(8,128)} %convert_element_type.149), channel_id=1, source_target_pairs={{0,2},{1,3},{2,0},{3,1},{4,6},{5,7},{6,4},{7,5},{8,10},{9,11},{10,... | collective-permute-start | bytes 3145736 | tf_op jit(solution)/shard_map/ppermute | solution.py:20
  10.5 28.6 %collective-permute-start.4 = (f32[8,256]{1,0:T(8,128)S(1)}, f32[8,256]{1,0:T(8,128)S(1)}, u32[]{:S(2)}, u32[]{:S(2)}) collective-permute-start(f32[8,256]{1,0:T(8,128)S(1)} %fusion.71), channel_id=1, source_target_pairs={{4,0},{8,4},{12,8},{16,12},{20,16},{24,20},{28,24},{5,1},{9,5},{13... | collective-permute-start | bytes 24584 | tf_op jit(solution)/shard_map/ppermute | solution.py:16
  32.1 24.8 %collective-permute-start.1 = (f32[1024,256]{1,0:T(8,128)S(1)}, f32[1024,256]{1,0:T(8,128)S(1)}, u32[]{:S(2)}, u32[]{:S(2)}) collective-permute-start(f32[1024,256]{1,0:T(8,128)S(1)} %dynamic-slice_convert_fusion), channel_id=1, source_target_pairs={{0,2},{1,3},{2,0},{3,1},{4,6},{5,7},{6,4},{7,5},{8,10},{9,11},{10,... | collective-permute-start | bytes 3145736 | tf_op jit(solution)/shard_map/ppermute | solution.py:20
  67.9 31.9 %collective-permute-start.10 = (f32[256,1024]{1,0:T(8,128)S(1)}, f32[256,1024]{1,0:T(8,128)}, u32[]{:S(2)}, u32[]{:S(2)}) collective-permute-start(f32[256,1024]{1,0:T(8,128)S(1)} %get-tuple-element.706.refs_0_), channel_id=1, source_target_pairs={{0,2},{1,3},{2,0},{3,1},{4,6},{5,7},{6,4},{7,5},{8,10},{9,11},{10,... | collective-permute-start | bytes 3145736 | tf_op jit(solution)/shard_map/ppermute | solution.py:20
  100.6 26.4 %collective-permute-start.15 = (f32[256,1024]{1,0:T(8,128)}, f32[256,1024]{1,0:T(8,128)}, u32[]{:S(2)}, u32[]{:S(2)}) collective-permute-start(f32[256,1024]{1,0:T(8,128)} %copy-done.57), channel_id=1, source_target_pairs={{0,2},{1,3},{2,0},{3,1},{4,6},{5,7},{6,4},{7,5},{8,10},{9,11},{10,... | collective-permute-start | bytes 3145736 | tf_op jit(solution)/shard_map/ppermute | solution.py:20
  100.9 25.7 %collective-permute-start.9 = (f32[512,1024]{1,0:T(8,128)}, f32[512,1024]{1,0:T(8,128)S(1)}, u32[]{:S(2)}, u32[]{:S(2)}) collective-permute-start(f32[512,1024]{1,0:T(8,128)} %get-tuple-element.348), channel_id=1, source_target_pairs={{0,1},{1,0},{2,3},{3,2},{4,5},{5,4},{6,7},{7,6},{8,9},{9,8},{10,11... | collective-permute-start | bytes 6291464 | tf_op jit(solution)/shard_map/ppermute | solution.py:20
  129.3 28.4 %collective-permute-start.14 = (f32[256,1024]{1,0:T(8,128)}, f32[256,1024]{1,0:T(8,128)}, u32[]{:S(2)}, u32[]{:S(2)}) collective-permute-start(f32[256,1024]{1,0:T(8,128)} %maximum_add_fusion.2), channel_id=1, source_target_pairs={{0,2},{1,3},{2,0},{3,1},{4,6},{5,7},{6,4},{7,5},{8,10},{9,11},{10,... | collective-permute-start | bytes 3145736 | tf_op jit(solution)/shard_map/ppermute | solution.py:20
  175.5 30.5 %collective-permute-start.20 = (f32[256,1024]{1,0:T(8,128)}, f32[256,1024]{1,0:T(8,128)}, u32[]{:S(2)}, u32[]{:S(2)}) collective-permute-start(f32[256,1024]{1,0:T(8,128)} %maximum_add_fusion.3), channel_id=1, source_target_pairs={{0,2},{1,3},{2,0},{3,1},{4,6},{5,7},{6,4},{7,5},{8,10},{9,11},{10,... | collective-permute-start | bytes 3145736 | tf_op jit(solution)/shard_map/ppermute | solution.py:20
  181.4 31.2 %collective-permute-start.24 = (f32[512,256]{1,0:T(8,128)}, f32[512,256]{1,0:T(8,128)}, u32[]{:S(2)}, u32[]{:S(2)}) collective-permute-start(f32[512,256]{1,0:T(8,128)} %fusion.121), channel_id=1, source_target_pairs={{0,2},{1,3},{2,0},{3,1},{4,6},{5,7},{6,4},{7,5},{8,10},{9,11},{10,... | collective-permute-start | bytes 1572872 | tf_op jit(solution)/shard_map/ppermute | solution.py:20
  199.7 58.7 %collective-permute-start.29 = (f32[4,128,1152]{2,1,0:T(8,128)}, f32[4,128,1152]{2,1,0:T(8,128)}, u32[]{:S(2)}, u32[]{:S(2)}) collective-permute-start(f32[4,128,1152]{2,1,0:T(8,128)} %bitcast.110), channel_id=1, source_target_pairs={{0,4},{4,0},{8,12},{12,8},{16,20},{20,16},{24,28},{28,24},{1,5},{5... | collective-permute-start | bytes 7077896 | tf_op jit(solution)/shard_map/ppermute | solution.py:20
  203.4 55.0 %collective-permute-start.30 = (f32[4,128,1152]{2,1,0:T(8,128)}, f32[4,128,1152]{2,1,0:T(8,128)}, u32[]{:S(2)}, u32[]{:S(2)}) collective-permute-start(f32[4,128,1152]{2,1,0:T(8,128)} %bitcast.15), channel_id=1, source_target_pairs={{0,8},{4,12},{8,0},{12,4},{16,24},{20,28},{24,16},{28,20},{1,9},{5... | collective-permute-start | bytes 7077896 | tf_op jit(solution)/shard_map/ppermute | solution.py:20
  238.5 61.3 %collective-permute-start.34 = (f32[256,1024]{1,0:T(8,128)}, f32[256,1024]{1,0:T(8,128)}, u32[]{:S(2)}, u32[]{:S(2)}) collective-permute-start(f32[256,1024]{1,0:T(8,128)} %add.565), channel_id=1, source_target_pairs={{0,2},{1,3},{2,0},{3,1},{4,6},{5,7},{6,4},{7,5},{8,10},{9,11},{10,... | collective-permute-start | bytes 3145736 | tf_op jit(solution)/shard_map/ppermute | solution.py:20
  245.1 45.2 %collective-permute-start.33 = (f32[256,1024]{1,0:T(8,128)}, f32[256,1024]{1,0:T(8,128)}, u32[]{:S(2)}, u32[]{:S(2)}) collective-permute-start(f32[256,1024]{1,0:T(8,128)} %add.566), channel_id=1, source_target_pairs={{0,2},{1,3},{2,0},{3,1},{4,6},{5,7},{6,4},{7,5},{8,10},{9,11},{10,... | collective-permute-start | bytes 3145736 | tf_op jit(solution)/shard_map/ppermute | solution.py:20
  262.7 28.8 %collective-permute-start.32 = (f32[2,128,1152]{2,1,0:T(8,128)}, f32[2,128,1152]{2,1,0:T(8,128)}, u32[]{:S(2)}, u32[]{:S(2)}) collective-permute-start(f32[2,128,1152]{2,1,0:T(8,128)} %get-tuple-element.482), channel_id=1, source_target_pairs={{0,8},{4,12},{8,0},{12,4},{16,24},{20,28},{24,16},{28,20},{1,9},{5... | collective-permute-start | bytes 3538952 | tf_op jit(solution)/shard_map/ppermute | solution.py:20
  264.4 59.3 %collective-permute-start.35 = (f32[4,128,1152]{2,1,0:T(8,128)}, f32[4,128,1152]{2,1,0:T(8,128)}, u32[]{:S(2)}, u32[]{:S(2)}) collective-permute-start(f32[4,128,1152]{2,1,0:T(8,128)} %bitcast.19), channel_id=1, source_target_pairs={{0,4},{4,0},{8,12},{12,8},{16,20},{20,16},{24,28},{28,24},{1,5},{5... | collective-permute-start | bytes 7077896 | tf_op jit(solution)/shard_map/ppermute | solution.py:20
  291.5 26.4 %collective-permute-start.36 = (f32[256,1024]{1,0:T(8,128)}, f32[256,1024]{1,0:T(8,128)}, u32[]{:S(2)}, u32[]{:S(2)}) collective-permute-start(f32[256,1024]{1,0:T(8,128)} %fusion.38), channel_id=1, source_target_pairs={{0,2},{1,3},{2,0},{3,1},{4,6},{5,7},{6,4},{7,5},{8,10},{9,11},{10,... | collective-permute-start | bytes 3145736 | tf_op jit(solution)/shard_map/ppermute | solution.py:20
  295.9 44.4 %collective-permute-start.39 = (f32[256,1024]{1,0:T(8,128)}, f32[256,1024]{1,0:T(8,128)}, u32[]{:S(2)}, u32[]{:S(2)}) collective-permute-start(f32[256,1024]{1,0:T(8,128)} %fusion.34), channel_id=1, source_target_pairs={{0,2},{1,3},{2,0},{3,1},{4,6},{5,7},{6,4},{7,5},{8,10},{9,11},{10,... | collective-permute-start | bytes 3145736 | tf_op jit(solution)/shard_map/ppermute | solution.py:20
  297.2 53.9 %collective-permute-start.42 = (f32[1,128,1152]{2,1,0:T(8,128)}, f32[1,128,1152]{2,1,0:T(8,128)}, u32[]{:S(2)}, u32[]{:S(2)}) collective-permute-start(f32[1,128,1152]{2,1,0:T(8,128)} %get-tuple-element.524), channel_id=1, source_target_pairs={{0,16},{4,20},{8,24},{12,28},{16,0},{20,4},{24,8},{28,12},{1,17},{... | collective-permute-start | bytes 1769480 | tf_op jit(solution)/shard_map/ppermute | solution.py:20
  323.7 45.7 %collective-permute-start.37 = (f32[4,128,768]{2,1,0:T(8,128)}, f32[4,128,768]{2,1,0:T(8,128)}, u32[]{:S(2)}, u32[]{:S(2)}) collective-permute-start(f32[4,128,768]{2,1,0:T(8,128)} %bitcast.26), channel_id=1, source_target_pairs={{0,4},{4,0},{8,12},{12,8},{16,20},{20,16},{24,28},{28,24},{1,5},{5... | collective-permute-start | bytes 4718600 | tf_op jit(solution)/shard_map/ppermute | solution.py:20
  326.1 43.3 %collective-permute-start.38 = (f32[256,1024]{1,0:T(8,128)}, f32[256,1024]{1,0:T(8,128)}, u32[]{:S(2)}, u32[]{:S(2)}) collective-permute-start(f32[256,1024]{1,0:T(8,128)} %fusion.24.refs_0_), channel_id=1, source_target_pairs={{0,2},{1,3},{2,0},{3,1},{4,6},{5,7},{6,4},{7,5},{8,10},{9,11},{10,... | collective-permute-start | bytes 3145736 | tf_op jit(solution)/shard_map/ppermute | solution.py:20
  340.3 25.7 %collective-permute-start.41 = (f32[2,128,1152]{2,1,0:T(8,128)}, f32[2,128,1152]{2,1,0:T(8,128)}, u32[]{:S(2)}, u32[]{:S(2)}) collective-permute-start(f32[2,128,1152]{2,1,0:T(8,128)} %get-tuple-element.523), channel_id=1, source_target_pairs={{0,8},{4,12},{8,0},{12,4},{16,24},{20,28},{24,16},{28,20},{1,9},{5... | collective-permute-start | bytes 3538952 | tf_op jit(solution)/shard_map/ppermute | solution.py:20
  351.0 50.1 %collective-permute-start.46 = (f32[256,1024]{1,0:T(8,128)}, f32[256,1024]{1,0:T(8,128)}, u32[]{:S(2)}, u32[]{:S(2)}) collective-permute-start(f32[256,1024]{1,0:T(8,128)} %fusion.19.refs_1_), channel_id=1, source_target_pairs={{0,2},{1,3},{2,0},{3,1},{4,6},{5,7},{6,4},{7,5},{8,10},{9,11},{10,... | collective-permute-start | bytes 3145736 | tf_op jit(solution)/shard_map/ppermute | solution.py:20
  373.1 28.9 %collective-permute-start.45 = (f32[2,128,768]{2,1,0:T(8,128)}, f32[2,128,768]{2,1,0:T(8,128)S(1)}, u32[]{:S(2)}, u32[]{:S(2)}) collective-permute-start(f32[2,128,768]{2,1,0:T(8,128)} %get-tuple-element.544), channel_id=1, source_target_pairs={{0,8},{4,12},{8,0},{12,4},{16,24},{20,28},{24,16},{28,20},{1,9},{5... | collective-permute-start | bytes 2359304 | tf_op jit(solution)/shard_map/ppermute | solution.py:20
  375.6 25.6 %collective-permute-start.47 = (f32[1,128,1152]{2,1,0:T(8,128)S(1)}, f32[1,128,1152]{2,1,0:T(8,128)S(1)}, u32[]{:S(2)}, u32[]{:S(2)}) collective-permute-start(f32[1,128,1152]{2,1,0:T(8,128)S(1)} %copy-done.121), channel_id=1, source_target_pairs={{0,16},{4,20},{8,24},{12,28},{16,0},{20,4},{24,8},{28,12},{1,17},{... | collective-permute-start | bytes 1769480 | tf_op jit(solution)/shard_map/ppermute | solution.py:20
  378.9 32.6 %collective-permute-start.43 = (f32[2,128,1152]{2,1,0:T(8,128)}, f32[2,128,1152]{2,1,0:T(8,128)}, u32[]{:S(2)}, u32[]{:S(2)}) collective-permute-start(f32[2,128,1152]{2,1,0:T(8,128)} %get-tuple-element.536), channel_id=1, source_target_pairs={{0,4},{4,0},{8,12},{12,8},{16,20},{20,16},{24,28},{28,24},{1,5},{5... | collective-permute-start | bytes 3538952 | tf_op jit(solution)/shard_map/ppermute | solution.py:20
  380.4 25.5 %collective-permute-start.44 = (f32[22,128]{1,0:T(8,128)}, f32[22,128]{1,0:T(8,128)}, u32[]{:S(2)}, u32[]{:S(2)}) collective-permute-start(f32[22,128]{1,0:T(8,128)} %pad_maximum_fusion.8), channel_id=1, source_target_pairs={{0,4},{4,0},{8,12},{12,8},{16,20},{20,16},{24,28},{28,24},{1,5},{5... | collective-permute-start | bytes 33800 | tf_op jit(solution)/shard_map/ppermute | solution.py:20
  401.2 23.6 %collective-permute-start.50 = (f32[256,1024]{1,0:T(8,128)}, f32[256,1024]{1,0:T(8,128)}, u32[]{:S(2)}, u32[]{:S(2)}) collective-permute-start(f32[256,1024]{1,0:T(8,128)} %get-tuple-element.564), channel_id=1, source_target_pairs={{0,2},{1,3},{2,0},{3,1},{4,6},{5,7},{6,4},{7,5},{8,10},{9,11},{10,... | collective-permute-start | bytes 3145736 | tf_op jit(solution)/shard_map/ppermute | solution.py:20
  423.2 29.7 %collective-permute-start.56 = (f32[512,1024]{1,0:T(8,128)}, f32[512,1024]{1,0:T(8,128)}, u32[]{:S(2)}, u32[]{:S(2)}) collective-permute-start(f32[512,1024]{1,0:T(8,128)} %pad_maximum_fusion.5), channel_id=1, source_target_pairs={{0,1},{1,0},{2,3},{3,2},{4,5},{5,4},{6,7},{7,6},{8,9},{9,8},{10,11... | collective-permute-start | bytes 6291464 | tf_op jit(solution)/shard_map/ppermute | solution.py:20
  424.4 28.5 %collective-permute-start.48 = (f32[1,128,1152]{2,1,0:T(8,128)}, f32[1,128,1152]{2,1,0:T(8,128)}, u32[]{:S(2)}, u32[]{:S(2)}) collective-permute-start(f32[1,128,1152]{2,1,0:T(8,128)} %get-tuple-element.561), channel_id=1, source_target_pairs={{0,16},{4,20},{8,24},{12,28},{16,0},{20,4},{24,8},{28,12},{1,17},{... | collective-permute-start | bytes 1769480 | tf_op jit(solution)/shard_map/ppermute | solution.py:20
  437.8 24.0 %collective-permute-start.55 = (f32[2,128,512]{2,1,0:T(8,128)}, f32[2,128,512]{2,1,0:T(8,128)S(1)}, u32[]{:S(2)}, u32[]{:S(2)}) collective-permute-start(f32[2,128,512]{2,1,0:T(8,128)} %get-tuple-element.580), channel_id=1, source_target_pairs={{0,8},{4,12},{8,0},{12,4},{16,24},{20,28},{24,16},{28,20},{1,9},{5... | collective-permute-start | bytes 1572872 | tf_op jit(solution)/shard_map/ppermute | solution.py:20
  440.8 24.5 %collective-permute-start.57 = (f32[256,1024]{1,0:T(8,128)}, f32[256,1024]{1,0:T(8,128)}, u32[]{:S(2)}, u32[]{:S(2)}) collective-permute-start(f32[256,1024]{1,0:T(8,128)} %get-tuple-element.594), channel_id=1, source_target_pairs={{0,2},{1,3},{2,0},{3,1},{4,6},{5,7},{6,4},{7,5},{8,10},{9,11},{10,... | collective-permute-start | bytes 3145736 | tf_op jit(solution)/shard_map/ppermute | solution.py:20
  (155 other events, 1566.4 us)
